TPU v7x, 256 devices: a whole 4x4x8 slice. The times are simulated.
256 devices in a mesh: band: 32 (over y, z_hi, core), grid: 8 (over z_lo, x).
Axes of the slice: x: 4, y: 4, z: 8 (z_hi: 4, z_lo: 2; z = z_hi * 2 + z_lo), core: 2. Of those that a mesh axis runs over, the one named last changes fastest.
Arguments:
- orbitals: float32 [128, 64, 80, 128], P('band', 'grid'), as said below
- potential: float32 [64, 80, 128], P('grid'), may hold values from -2 to 1
- projectors: float32 [4, 16384], P(None, 'grid'), may hold values from -3 to 3
- coupling: float32 [64, 4, 4], P('grid'), may hold values from -4 to 4
- entry_cell: int32 [16384], P('grid'), may hold values from 0 to 81919
- entry_atom: int32 [16384], P('grid'), may hold values from -1 to 63, as said below
Outputs:
- block_out: float32 [128, 64, 80, 128], P('band', 'grid')
Inputs may be any that keep to these rules, and one draw needn't show every extreme that they name: `entry_atom`: atoms a*8 to (a+1)*8 - 1 belong to domain a. A live slot of domain g names an atom of domain g-1, g or g+1; a domain's live slots come first; one domain has all 2048 slots live and another only 512 in every draw, the others 2048/4, 1024, 1536 or 2048. Each orbital is its own rough field plus a multiple of one field common to all orbitals, scaled per orbital.
All inputs are finite; a program needn't handle non-finite values.
Results may differ from a plain program's by a relative error of at most 0.00019.
Values sent between devices are 32-bit elements; how exact they have to be, the bound alone decides.
A program may use at most 128 MiB of HBM per device.

v0:
```python
import math

import jax
import jax.numpy as jnp
from jax import lax
from jax.sharding import PartitionSpec as P

ATOM_DEV = 8


CENTER = 34.0
HALF = 30.0
SPACING = 0.5
REACH = 6


def padded_2(cells, sides, width):
    for axis, dim in sides:
        count = lax.axis_size(axis)
        ends = count - 1
        head = lax.slice_in_dim(cells, 0, width, axis=dim)
        tail = lax.slice_in_dim(cells, cells.shape[dim] - width, cells.shape[dim], axis=dim)
        cells = jnp.concatenate(
            [
                lax.ppermute(tail, axis, [(i, (i + 1) % count) for i in range(ends)]),
                cells,
                lax.ppermute(head, axis, [((i + 1) % count, i) for i in range(ends)]),
            ],
            axis=dim,
        )
    return cells


def from_root(array, axis, root):
    mine = lax.axis_index(axis) == root
    return lax.psum(jnp.where(mine, array, jnp.zeros_like(array)), axis)


def stencil_weights():
    factorial_of = math.factorial
    side_weights = [
        2.0
        * (-1.0) ** (k + 1)
        * factorial_of(REACH) ** 2
        / (k * k * factorial_of(REACH - k) * factorial_of(REACH + k))
        for k in range(1, REACH + 1)
    ]
    return (-2.0 * sum(side_weights), side_weights)


def kinetic(padded, shape):
    center, side_weights = stencil_weights()
    size_x, size_y, size_z = (shape[1], shape[2], shape[3])
    inner = padded[:, REACH : REACH + size_x, REACH : REACH + size_y, REACH : REACH + size_z]
    total = 3.0 * center * inner
    for k in range(1, REACH + 1):
        weight = side_weights[k - 1]
        plus_x = padded[
            :, REACH + k : REACH + k + size_x, REACH : REACH + size_y, REACH : REACH + size_z
        ]
        minus_x = padded[
            :, REACH - k : REACH - k + size_x, REACH : REACH + size_y, REACH : REACH + size_z
        ]
        plus_y = padded[
            :, REACH : REACH + size_x, REACH + k : REACH + k + size_y, REACH : REACH + size_z
        ]
        minus_y = padded[
            :, REACH : REACH + size_x, REACH - k : REACH - k + size_y, REACH : REACH + size_z
        ]
        plus_z = padded[
            :, REACH : REACH + size_x, REACH : REACH + size_y, REACH + k : REACH + k + size_z
        ]
        minus_z = padded[
            :, REACH : REACH + size_x, REACH : REACH + size_y, REACH - k : REACH - k + size_z
        ]
        total = total + weight * (plus_x + minus_x + plus_y + minus_y + plus_z + minus_z)
    return -0.5 / (SPACING * SPACING) * total


def nonlocal_term(flat_field, projectors, coupling_rows, entry_cell, entry_atom):
    highest = lax.Precision.HIGHEST
    atom_count = ATOM_DEV * lax.axis_size("grid")
    values = flat_field[:, entry_cell]
    onehot = (entry_atom[:, None] == jnp.arange(atom_count, dtype=jnp.int32)[None, :]).astype(
        jnp.float32
    )
    weighted = projectors[:, None, :] * values[None]
    partial_sums = jnp.einsum("jbe,ea->ajb", weighted, onehot, precision=highest)
    projector_coeffs = lax.psum(partial_sums, "grid")
    grid_index = lax.axis_index("grid")
    padded_coeffs = jnp.pad(projector_coeffs, ((ATOM_DEV, ATOM_DEV), (0, 0), (0, 0)))
    near_coeffs = lax.dynamic_slice_in_dim(padded_coeffs, grid_index * ATOM_DEV, 3 * ATOM_DEV, 0)
    near_mixed = jnp.einsum("aij,ajb->aib", coupling_rows, near_coeffs, precision=highest)
    local_atom = jnp.where(entry_atom >= 0, entry_atom - (grid_index - 1) * ATOM_DEV, -1)
    near_onehot = (
        local_atom[:, None] == jnp.arange(3 * ATOM_DEV, dtype=jnp.int32)[None, :]
    ).astype(jnp.float32)
    picked = jnp.einsum("ea,aib->ibe", near_onehot, near_mixed, precision=highest)
    back_values = jnp.sum(projectors[:, None, :] * picked, axis=0)
    result = jnp.zeros(flat_field.shape, jnp.float32)
    return result.at[:, entry_cell].add(back_values)


def apply_hamiltonian(group, potential, projectors, coupling_rows, entry_cell, entry_atom):
    extended = padded_2(group, (("grid", 1),), REACH)
    padded = jnp.pad(extended, ((0, 0), (0, 0), (REACH, REACH), (REACH, REACH)))
    kinetic_part = kinetic(padded, group.shape)
    flat_field = group.reshape(group.shape[0], -1)
    nonlocal_part = nonlocal_term(
        flat_field, projectors, coupling_rows, entry_cell, entry_atom
    ).reshape(group.shape)
    return kinetic_part + potential[None] * group + nonlocal_part


def orthonormal(panel, cell_total):
    highest = lax.Precision.HIGHEST
    local_gram = jnp.dot(panel, panel.T, precision=highest, preferred_element_type=jnp.float32)
    gram_matrix = lax.psum(local_gram, "grid") / cell_total
    factor_lower = jnp.linalg.cholesky(gram_matrix)
    return jax.scipy.linalg.solve_triangular(factor_lower, panel, lower=True)


def local(orbitals, potential, projectors, coupling, entry_cell, entry_atom):
    highest = lax.Precision.HIGHEST
    coupling_rows = padded_2(coupling, (("grid", 0),), ATOM_DEV)
    first = apply_hamiltonian(
        orbitals, potential, projectors, coupling_rows, entry_cell, entry_atom
    )
    filtered_one = (first - CENTER * orbitals) / HALF
    second = apply_hamiltonian(
        filtered_one, potential, projectors, coupling_rows, entry_cell, entry_atom
    )
    filtered = 2.0 * (second - CENTER * filtered_one) / HALF - orbitals
    flat_field = filtered.reshape(filtered.shape[0], -1)
    cell_total = flat_field.shape[1] * lax.axis_size("grid")
    own_basis = orthonormal(flat_field, cell_total)
    panel_basis = from_root(own_basis, "band", 0)
    local_correlations = jnp.dot(
        panel_basis, flat_field.T, precision=highest, preferred_element_type=jnp.float32
    )
    correlations = lax.psum(local_correlations, "grid") / cell_total
    trailing = flat_field - jnp.dot(
        correlations.T, panel_basis, precision=highest, preferred_element_type=jnp.float32
    )
    result = jnp.where(lax.axis_index("band") == 0, panel_basis, trailing)
    return result.reshape(orbitals.shape)


def solution(mesh):
    return jax.shard_map(
        local,
        mesh=mesh,
        in_specs=(
            P("band", "grid", None, None),
            P("grid", None, None),
            P(None, "grid"),
            P("grid", None, None),
            P("grid"),
            P("grid"),
        ),
        out_specs=P("band", "grid", None, None),
        check_vma=False,
    )
```

profile of v0, /device:TPU:32, one launch (start us, length us, event | category | flops | bytes accessed | tf_op | source)
XLA Modules:
  0.0 687.5 jit_solution(1141499058745075133)
XLA Ops:
  6.5 4.3 collective-permute-start.3
  10.9 1.9 collective-permute-start.2
  12.8 2.9 fusion.125
  15.7 6.0 collective-permute-start
  21.8 1.9 collective-permute-start.1
  23.7 19.1 %copy.20 = f32[4,8,80,128]{0,3,2,1:T(8,128)} copy(f32[4,8,80,128]{3,2,1,0:T(8,128)S(1)} %copy-done) | data formatting | bytes 2621440 | tf_op args[0]
  42.9 20.6 %gather_fusion = f32[2048,4]{1,0:T(8,128)} fusion(f32[4,81920]{0,1:T(8,128)} %bitcast.46, s32[2048]{0:T(1024)S(1)} %get-tuple-element.13), kind=kCustom, calls=%fused_computation | custom fusion | bytes 73728 | tf_op jit(solution)/shard_map/gather | solution.py:83
  63.5 1.6 copy.21
  65.0 0.6 fusion.92
  65.8 0.6 subtract_select_fusion
  66.4 35.9 %psum.35 = f32[64,4,4]{2,1,0:T(4,128)S(1)} all-reduce(f32[64,4,4]{2,1,0:T(4,128)S(1)} %copy.35), channel_id=1, replica_groups=mesh['band'=32,'grid'=8] {'grid'}, use_global_device_ids=true, to_apply=%region_0.1 | all-reduce | flops 1024 | bytes 8192 | tf_op jit(solution)/shard_map/psum | solution.py:89
  102.4 0.8 pad_maximum_fusion.2
  103.6 1.1 fusion.84
  104.7 1.3 copy.23
  106.1 28.7 %scatter_custom_fusion = f32[4,81920]{0,1:T(8,128)} fusion(s32[2048]{0:T(1024)S(1)} %get-tuple-element.14, f32[2048,4]{1,0:T(8,128)} %copy.23, f32[]{:T(128)} %constant.79.clone.1), kind=kCustom, calls=%fused_computation.9 | custom fusion | flops 8192 | bytes 1311232 | tf_op jit(solution)/shard_map/scatter-add | solution.py:101
  134.8 22.9 %copy.24 = f32[4,8,80,128]{3,2,1,0:T(8,128)} copy(f32[4,8,80,128]{0,3,2,1:T(8,128)} %bitcast.45) | data formatting | bytes 2621440 | tf_op jit(solution)/shard_map/reshape | solution.py:111
  158.1 1.4 copy-done.3
  159.4 3.1 select_maximum_fusion.2
  162.7 1.3 copy-done.2
  164.0 0.6 copy-done.6
  164.8 11.2 %broadcast_multiply_fusion = (f32[4,8,80,128]{3,2,1,0:T(8,128)S(1)}, f32[4,8,80,128]{3,2,1,0:T(8,128)}) fusion(f32[4,8,80,128]{3,2,1,0:T(8,128)S(1)} %copy-done, f32[4,8,80,128]{3,2,1,0:T(8,128)S(1)} %copy-done.6, f32[8,80,128]{2,1,0:T(8,128)S(1)} %copy-done.8, f32[4,20,92,140]{3,2,1,0:T(8,128)S(1)} %select_maximum_fusion.2, ...), kind=kLoop, calls=%fused_computation.165 | loop fusion | flops 16384000 | bytes 52756480 | tf_op jit(solution)/shard_map/div | solution.py:129
  176.0 1.6 fusion.124
  177.6 1.9 collective-permute-start.5
  179.5 6.0 collective-permute-start.4
  185.6 19.1 %copy.25 = f32[4,8,80,128]{0,3,2,1:T(8,128)} copy(f32[4,8,80,128]{3,2,1,0:T(8,128)S(1)} %get-tuple-element.5) | data formatting | bytes 2621440 | tf_op jit(solution)/shard_map/div | solution.py:129
  204.8 18.4 %gather_fusion.1 = f32[2048,4]{1,0:T(8,128)S(1)} fusion(f32[4,81920]{0,1:T(8,128)} %bitcast.47, s32[2048]{0:T(1024)S(1)} %get-tuple-element.13), kind=kCustom, calls=%fused_computation.1 | custom fusion | bytes 73728 | tf_op jit(solution)/shard_map/gather | solution.py:83
  223.2 0.3 copy.26
  223.6 0.6 fusion.90
  224.3 31.8 %psum.36 = f32[64,4,4]{2,1,0:T(4,128)S(1)} all-reduce(f32[64,4,4]{2,1,0:T(4,128)S(1)} %copy.38), channel_id=1, replica_groups=mesh['band'=32,'grid'=8] {'grid'}, use_global_device_ids=true, to_apply=%region_3.4 | all-reduce | flops 1024 | bytes 8192 | tf_op jit(solution)/shard_map/psum | solution.py:89
  256.4 0.3 fusion.85
  256.7 0.4 copy.28
  257.1 28.1 %scatter_custom_fusion.1 = f32[4,81920]{0,1:T(8,128)} fusion(s32[2048]{0:T(1024)S(1)} %get-tuple-element.14, f32[2048,4]{1,0:T(8,128)S(1)} %copy.28, f32[]{:T(128)} %constant.79.clone.1), kind=kCustom, calls=%fused_computation.7 | custom fusion | flops 8192 | bytes 1310724 | tf_op jit(solution)/shard_map/scatter-add | solution.py:101
  285.2 22.9 %copy.29 = f32[4,8,80,128]{3,2,1,0:T(8,128)} copy(f32[4,8,80,128]{0,3,2,1:T(8,128)} %bitcast.44) | data formatting | bytes 2621440 | tf_op jit(solution)/shard_map/reshape | solution.py:111
  308.2 1.0 copy-done.7
  309.1 4.4 select_maximum_fusion
  313.5 15.8 %fusion.23 = f32[4,8,80,128]{3,2,1,0:T(8,128)} fusion(f32[4,8,80,128]{3,2,1,0:T(8,128)} %param.6, f32[4,8,80,128]{3,2,1,0:T(8,128)} %copy.29, f32[4,8,80,128]{3,2,1,0:T(8,128)} %copy-done.1, f32[4,6,80,128]{3,2,1,0:T(8,128)} %copy-done.7, f32[4,6,80,128]{3,2,1,0:T(8,128)} %collective-permute-done.4, f32[4,20,92,140]{3,2,1,0:T(8,128)S(1)} %select_maximum_fusion, ...), kind=kLoop, calls=%fused_computation.59 | loop fusion | flops 20643840 | bytes 40304640 | tf_op jit(solution)/shard_map/sub | solution.py:133
  329.3 8.6 %fusion.86 = f32[4,4]{0,1:T(4,128)S(1)} fusion(f32[4,8,80,128]{3,2,1,0:T(8,128)} %fusion.23), kind=kOutput, calls=%fused_computation.158 | convolution fusion | flops 15728640 | bytes 1310784 | tf_op jit(solution)/shard_map/dot_general | solution.py:117
  337.9 18.1 %psum.37 = f32[4,4]{0,1:T(4,128)S(1)} all-reduce(f32[4,4]{0,1:T(4,128)S(1)} %fusion.86), channel_id=1, replica_groups=mesh['band'=32,'grid'=8] {'grid'}, use_global_device_ids=true, to_apply=%region_6.7 | all-reduce | flops 16 | bytes 128 | tf_op jit(solution)/shard_map/psum | solution.py:118
  356.2 0.4 cholesky.16
  356.6 0.7 compare_reduce_fusion
  357.3 0.7 fusion.113
  358.0 0.3 custom-call.7
  358.3 4.6 convolution_select_fusion
  363.0 286.9 %all-reduce.6.cloned.1.call-done = f32[4,81920]{1,0:T(4,128)} async-done(((f32[4,81920]{1,0:T(4,128)}), f32[4,81920]{1,0:T(4,128)}) %all-reduce.6.cloned.1.call-update) | async-done | bytes 1310736 | tf_op jit(solution)/shard_map/psum | solution.py:36
  649.9 7.3 %fusion.61 = f32[4,4]{0,1:T(4,128)S(1)} fusion(f32[4,81920]{1,0:T(4,128)} %all-reduce.6.cloned.1.call-done, f32[1,4,640,128]{3,2,1,0:T(8,128)S(1)} %bitcast.49), kind=kOutput, calls=%fused_computation.97 | convolution fusion | flops 15728640 | bytes 2621504 | tf_op jit(solution)/shard_map/dot_general | solution.py:138
  657.2 19.0 %psum.39 = f32[4,4]{0,1:T(4,128)S(1)} all-reduce(f32[4,4]{0,1:T(4,128)S(1)} %fusion.61), channel_id=1, replica_groups=mesh['band'=32,'grid'=8] {'grid'}, use_global_device_ids=true, to_apply=%region_10.11 | all-reduce | flops 16 | bytes 128 | tf_op jit(solution)/shard_map/psum | solution.py:141
  676.2 3.1 fusion.8
  679.3 1.1 copy.50
  (48 shorter events, 1.7 us)
Async XLA Ops:
  6.5 17.2 %copy-start = (f32[4,8,80,128]{3,2,1,0:T(8,128)S(1)}, f32[4,8,80,128]{3,2,1,0:T(8,128)}, u32[]{:S(2)}) copy-start(f32[4,8,80,128]{3,2,1,0:T(8,128)} %param.6) | copy-start | bytes 3932164
  6.5 17.2 %copy-start.9 = (s32[2048]{0:T(1024)S(1)}, s32[2048]{0:T(1024)}, u32[]{:S(2)}) copy-start(s32[2048]{0:T(1024)} %param.10) | copy-start | bytes 24580
  6.5 643.4 %all-reduce.6.cloned.1.call-start = ((), (), s32[]{:S(2)}) async-start(), calls=%async_computation | async-start | bytes 2621440 | tf_op jit(solution)/shard_map/psum | solution.py:36
  6.5 95.8 %collective-permute-start.3 = (f32[8,4,4]{0,2,1:T(4,128)}, f32[8,4,4]{0,2,1:T(4,128)}, u32[]{:S(2)}, u32[]{:S(2)}) collective-permute-start(f32[8,4,4]{0,2,1:T(4,128)} %param.9), channel_id=1, source_target_pairs={{1,0},{2,1},{3,2},{4,3},{5,4},{6,5},{7,6},{9,8},{10,9},{11,10},{12... | collective-permute-start | bytes 1544 | tf_op jit(solution)/shard_map/ppermute | solution.py:27
  10.9 91.5 %collective-permute-start.2 = (f32[8,4,4]{0,2,1:T(4,128)}, f32[8,4,4]{0,2,1:T(4,128)}, u32[]{:S(2)}, u32[]{:S(2)}) collective-permute-start(f32[8,4,4]{0,2,1:T(4,128)} %param.9), channel_id=1, source_target_pairs={{0,1},{1,2},{2,3},{3,4},{4,5},{5,6},{6,7},{8,9},{9,10},{10,11},{11... | collective-permute-start | bytes 1544 | tf_op jit(solution)/shard_map/ppermute | solution.py:25
  15.7 143.7 %collective-permute-start = (f32[4,6,80,128]{3,2,1,0:T(8,128)}, f32[4,6,80,128]{3,2,1,0:T(8,128)S(1)}, u32[]{:S(2)}, u32[]{:S(2)}) collective-permute-start(f32[4,6,80,128]{3,2,1,0:T(8,128)} %get-tuple-element.12), channel_id=1, source_target_pairs={{1,0},{2,1},{3,2},{4,3},{5,4},{6,5},{7,6},{9,8},{10,9},{11,10},{12... | collective-permute-start | bytes 2949128 | tf_op jit(solution)/shard_map/ppermute | solution.py:27
  21.8 136.0 %collective-permute-start.1 = (f32[4,6,80,128]{3,2,1,0:T(8,128)}, f32[4,6,80,128]{3,2,1,0:T(8,128)S(1)}, u32[]{:S(2)}, u32[]{:S(2)}) collective-permute-start(f32[4,6,80,128]{3,2,1,0:T(8,128)} %get-tuple-element.11), channel_id=1, source_target_pairs={{0,1},{1,2},{2,3},{3,4},{4,5},{5,6},{6,7},{8,9},{9,10},{10,11},{11... | collective-permute-start | bytes 2949128 | tf_op jit(solution)/shard_map/ppermute | solution.py:25
  42.9 22.2 %copy-start.10 = (s32[2048]{0:T(1024)S(1)}, s32[2048]{0:T(1024)}, u32[]{:S(2)}) copy-start(s32[2048]{0:T(1024)} %param.11) | copy-start | bytes 24580
  42.9 22.2 %copy-start.13 = (f32[4,2048]{1,0:T(4,128)S(1)}, f32[4,2048]{1,0:T(4,128)}, u32[]{:S(2)}) copy-start(f32[4,2048]{1,0:T(4,128)} %param.8) | copy-start | bytes 98308
  158.0 1.4 copy-start.3
  162.6 2.0 copy-start.6
  162.6 2.2 copy-start.8
  162.7 1.4 copy-start.2
  176.0 9.6 %copy-start.1 = (f32[4,8,80,128]{3,2,1,0:T(8,128)}, f32[4,8,80,128]{3,2,1,0:T(8,128)S(1)}, u32[]{:S(2)}) copy-start(f32[4,8,80,128]{3,2,1,0:T(8,128)S(1)} %get-tuple-element.5) | copy-start | bytes 3932164
  177.6 130.5 %collective-permute-start.5 = (f32[4,6,80,128]{3,2,1,0:T(8,128)}, f32[4,6,80,128]{3,2,1,0:T(8,128)S(1)}, u32[]{:S(2)}, u32[]{:S(2)}) collective-permute-start(f32[4,6,80,128]{3,2,1,0:T(8,128)} %get-tuple-element.8), channel_id=1, source_target_pairs={{0,1},{1,2},{2,3},{3,4},{4,5},{5,6},{6,7},{8,9},{9,10},{10,11},{11... | collective-permute-start | bytes 2949128 | tf_op jit(solution)/shard_map/ppermute | solution.py:25
  179.5 129.6 %collective-permute-start.4 = (f32[4,6,80,128]{3,2,1,0:T(8,128)}, f32[4,6,80,128]{3,2,1,0:T(8,128)}, u32[]{:S(2)}, u32[]{:S(2)}) collective-permute-start(f32[4,6,80,128]{3,2,1,0:T(8,128)} %get-tuple-element.7), channel_id=1, source_target_pairs={{1,0},{2,1},{3,2},{4,3},{5,4},{6,5},{7,6},{9,8},{10,9},{11,10},{12... | collective-permute-start | bytes 2949128 | tf_op jit(solution)/shard_map/ppermute | solution.py:27
  204.8 18.8 %copy-start.11 = (s32[2048]{0:T(1024)S(1)}, s32[2048]{0:T(1024)}, u32[]{:S(2)}) copy-start(s32[2048]{0:T(1024)} %param.11) | copy-start | bytes 24580
  204.8 18.8 %copy-start.14 = (f32[4,2048]{1,0:T(4,128)S(1)}, f32[4,2048]{1,0:T(4,128)}, u32[]{:S(2)}) copy-start(f32[4,2048]{1,0:T(4,128)} %param.8) | copy-start | bytes 98308
  223.2 33.2 %copy-start.12 = (s32[2048]{0:T(1024)S(1)}, s32[2048]{0:T(1024)}, u32[]{:S(2)}) copy-start(s32[2048]{0:T(1024)} %subtract_select_fusion) | copy-start | bytes 24580
  308.2 1.0 copy-start.7
  329.3 29.0 %copy-start.4 = (f32[4,8,80,128]{3,2,1,0:T(8,128)S(1)}, f32[4,8,80,128]{3,2,1,0:T(8,128)}, u32[]{:S(2)}) copy-start(f32[4,8,80,128]{3,2,1,0:T(8,128)} %fusion.23) | copy-start | bytes 3932164
  649.9 26.3 %copy-start.5 = (f32[4,81920]{1,0:T(4,128)S(1)}, f32[4,81920]{1,0:T(4,128)}, u32[]{:S(2)}) copy-start(f32[4,81920]{1,0:T(4,128)} %all-reduce.6.cloned.1.call-done) | copy-start | bytes 3932164
Sparse Core Ops, SparseCore 0:
  363.1 286.7 all-reduce.5
where the time goes:
time: 696 us; the launch traced here: 688 us
  waiting for transfers between devices  287 us (41%)
  local copies, waits for them, and re-layouts  138 us (20%)
  blocking collectives  105 us (15%)
  other arithmetic  94.9 us (14%)
  matrix products  26.9 us (4%)
  starting transfers between devices  22.1 us (3%)
  between operations  14 us (2%)
    psum x1, waiting for transfers between devices, from_root(): return lax.psum(jnp.where(mine, array, jnp.zeros_like(array)), axis)  287 us
    psum x2, blocking collectives, nonlocal_term(): projector_coeffs = lax.psum(partial_sums, 'grid')  67.7 us
    scatter-add x2, other arithmetic, nonlocal_term(): return result.at[:, entry_cell].add(back_values)  56.8 us
    reshape x2, local copies, waits for them, and re-layouts, apply_hamiltonian(): nonlocal_part = nonlocal_term(flat_field, projectors, coupling_rows, entr...  45.9 us
    gather x4, local copies, waits for them, and re-layouts, nonlocal_term(): values = flat_field[:, entry_cell]  40.9 us
    unnamed x34, local copies, waits for them, and re-layouts  25 us
    div x1, local copies, waits for them, and re-layouts, local(): filtered_one = (first - CENTER * orbitals) / HALF  19.1 us
    psum x1, blocking collectives, local(): correlations = lax.psum(local_correlations, 'grid') / cell_total  19 us
  transfers between devices with their start and end apart: 7, of which 1 were waited for; matrix products, arithmetic and copies ran while one was open for 28% of the time, Pallas kernels for 0%

commit v1 on v0

v1 whole, which is shorter than its diff:
```python
import functools
import math

import jax
import jax.numpy as jnp
from jax import lax
from jax.experimental import pallas as pl
from jax.experimental.pallas import tpu as pltpu
from jax.sharding import PartitionSpec as P

CENTER = 34.0
HALF = 30.0
SPACING = 0.5
REACH = 6
LANES = 128
ATOM_DEV = 8
GROUP = 32
TILE = 256
MESH = pl.DeviceIdType.MESH
COEF_STEPS = (-2, -1, 1, 2)


def stencil_weights():
    fact = math.factorial
    side = [
        2.0 * (-1.0) ** (k + 1) * fact(REACH) ** 2 / (k * k * fact(REACH - k) * fact(REACH + k))
        for k in range(1, REACH + 1)
    ]
    return -2.0 * sum(side), side


C0, CK = stencil_weights()
KIN = -0.5 / (SPACING * SPACING)
DIAG = (3.0 * KIN * C0 - CENTER) / HALF
EK = [KIN * c / HALF for c in CK]


def split(x):
    high = x.astype(jnp.bfloat16)
    return high, (x - high.astype(jnp.float32)).astype(jnp.bfloat16)


def dot(a, b):
    return jnp.dot(a, b, preferred_element_type=jnp.float32)


def kernel(
    n_band, n_grid, nx, ny, ent,
    orb_ref, pot_ref, proj_ref, cp_ref, cell_ref, atom_ref,
    out_ref,
    ext1, ext2, filt, panel, rows_m, rows_t, lane_m, m_row, m_col, picked, spread, vcat, acc,
    zmat, wcat, cols, coef_out, coef_in, coup_in, pairs, gram_out, gram_in,
    own_sem, halo_send, halo_recv, coef_send, coef_recv, coup_send, coup_recv,
    scat_send, scat_recv, gath_send, gath_recv, sib_send, sib_recv, copy_sem,
    gram_send, gram_recv,
):
    f32, bf16 = jnp.float32, jnp.bfloat16
    norb = orb_ref.shape[0]
    plane_rows = nx * ny
    reach_rows = REACH * ny
    chips = n_band // 2
    piece = plane_rows // chips
    band, grid = lax.axis_index("band"), lax.axis_index("grid")
    chip = lax.div(band, 2)
    core = lax.rem(band, 2)
    sibling = band + 1 - 2 * core
    main = core == 0
    has_left, has_right = grid > 0, grid < n_grid - 1

    def peer(step):
        return lax.rem(grid + step + n_grid, n_grid)

    barrier = pltpu.get_barrier_semaphore()
    for step in range(1, n_grid):
        pl.semaphore_signal(barrier, inc=1, device_id=(band, peer(step)), device_id_type=MESH)
    pl.semaphore_signal(barrier, inc=1, device_id=(sibling, grid), device_id_type=MESH)

    def other_chip(step):
        return 2 * lax.rem(chip + step, chips)

    @pl.when(main)
    def _():
        @pl.loop(1, chips)
        def _(step):
            pl.semaphore_signal(
                barrier, inc=1, device_id=(other_chip(step), grid), device_id_type=MESH
            )

        pl.semaphore_wait(barrier, n_grid + chips - 1)

    @pl.when(core == 1)
    def _():
        pl.semaphore_wait(barrier, n_grid)

    def halo(source, start, ext, b, app, side):
        step = -1 if side == 0 else 1
        first = start if side == 0 else start + plane_rows - reach_rows
        land = reach_rows + plane_rows if side == 0 else 0
        return pltpu.make_async_remote_copy(
            src_ref=source.at[b, pl.ds(first, reach_rows)],
            dst_ref=ext.at[b, pl.ds(land, reach_rows)],
            send_sem=halo_send.at[app, b, side],
            recv_sem=halo_recv.at[app, b, 1 - side],
            device_id=(band, grid + step),
            device_id_type=MESH,
        )

    def halo_source(app):
        return (orb_ref, 0, ext1) if app == 0 else (ext2, reach_rows, ext2)

    def send_halos(b, app):
        source, start, ext = halo_source(app)

        @pl.when(has_left)
        def _():
            halo(source, start, ext, b, app, 0).start()

        @pl.when(has_right)
        def _():
            halo(source, start, ext, b, app, 1).start()

    def wait_halos(b, app, sent):
        source, start, ext = halo_source(app)

        @pl.when(has_left)
        def _():
            if sent:
                halo(source, start, ext, b, app, 0).wait_send()
            else:
                halo(source, start, ext, b, app, 1).wait_recv()

        @pl.when(has_right)
        def _():
            if sent:
                halo(source, start, ext, b, app, 1).wait_send()
            else:
                halo(source, start, ext, b, app, 0).wait_recv()

    def own_copy(b):
        return pltpu.make_async_copy(
            orb_ref.at[b], ext1.at[b, pl.ds(reach_rows, plane_rows)], own_sem.at[b]
        )

    @pl.loop(0, norb)
    def _(b):
        send_halos(b, 0)
        own_copy(b).start()

    def coup_copy(k):
        return pltpu.make_async_remote_copy(
            src_ref=cp_ref, dst_ref=coup_in.at[k],
            send_sem=coup_send.at[k], recv_sem=coup_recv.at[k],
            device_id=(band, peer((-1, 1)[k])), device_id_type=MESH,
        )

    for k in range(2):
        coup_copy(k).start()

    zero_halo = jnp.zeros((norb, reach_rows, LANES), f32)
    for ext in (ext1, ext2):
        @pl.when(jnp.logical_not(has_left))
        def _():
            ext[:, 0:reach_rows] = zero_halo

        @pl.when(jnp.logical_not(has_right))
        def _():
            ext[:, reach_rows + plane_rows :] = zero_halo

    cell = cell_ref[...]
    atom = atom_ref[...]
    row_of = lax.shift_right_logical(cell, 7)
    lane_of = jnp.bitwise_and(cell, LANES - 1)
    near = jnp.where(atom >= 0, atom - (grid - 1) * ATOM_DEV, -1000)
    for j in range(4):
        hit = lax.broadcasted_iota(jnp.int32, (GROUP, ent), 0) == near
        high, low = split(jnp.where(hit, proj_ref[j : j + 1, :], 0.0))
        m_row[GROUP * j : GROUP * (j + 1)] = high
        m_row[LANES + GROUP * j : LANES + GROUP * (j + 1)] = low
    packed = jnp.concatenate(
        [row_of.astype(f32), lane_of.astype(f32), near.astype(f32), near.astype(f32), proj_ref[...]],
        axis=0,
    )
    cols[...] = packed.T

    @pl.loop(0, ent // TILE)
    def _(i):
        part = pl.ds(pl.multiple_of(i * TILE, TILE), TILE)
        column = cols[part, :]
        lane = lax.broadcasted_iota(jnp.int32, (TILE, LANES), 1).astype(f32)
        wide = lax.broadcasted_iota(jnp.int32, (TILE, plane_rows), 1).astype(f32)
        rows_m[part, :] = jnp.where(column[:, 0:1] == wide, 1.0, 0.0).astype(bf16)
        lane_m[part, :] = jnp.where(column[:, 1:2] == lane, 1.0, 0.0)
        total = jnp.zeros((TILE, LANES), f32)
        for j in range(4):
            total = jnp.where(column[:, 2:3] + (GROUP * j) == lane, column[:, 4 + j : 5 + j], total)
        high, low = split(total)
        m_col[part, 0:LANES] = high
        m_col[part, LANES:] = low

    @pl.loop(0, nx)
    def _(x):
        first = pl.multiple_of(x * ny, ny)
        down = lax.broadcasted_iota(jnp.int32, (ny, ent), 0) + first
        rows_t[pl.ds(first, ny), :] = jnp.where(down == row_of, 1.0, 0.0).astype(bf16)

    apart = jnp.abs(
        lax.broadcasted_iota(jnp.int32, (LANES, LANES), 0)
        - lax.broadcasted_iota(jnp.int32, (LANES, LANES), 1)
    )
    band_m = jnp.zeros((LANES, LANES), f32)
    for k in range(1, REACH + 1):
        band_m = jnp.where(apart == k, EK[k - 1], band_m)
    high, low = split(band_m)
    zmat[0:LANES, 0:LANES] = high
    zmat[0:LANES, LANES:] = low
    zmat[LANES:, 0:LANES] = high
    zmat[LANES:, LANES:] = jnp.zeros((LANES, LANES), bf16)

    def coef_copy(app, b, d):
        return pltpu.make_async_remote_copy(
            src_ref=coef_out.at[app, b], dst_ref=coef_in.at[app, b, d],
            send_sem=coef_send.at[app, b, d], recv_sem=coef_recv.at[app, b, d],
            device_id=(band, peer(COEF_STEPS[d])), device_id_type=MESH,
        )

    def cut(ext, b):
        for x in range(nx):
            high, low = split(ext[b, reach_rows + x * ny : reach_rows + (x + 1) * ny, :])
            vcat[b, x * ny : (x + 1) * ny, 0:LANES] = high
            vcat[b, x * ny : (x + 1) * ny, LANES:] = low

    def coefficients(ext, b, app):
        cut(ext, b)

        @pl.loop(0, ent // TILE)
        def _(i):
            part = pl.ds(pl.multiple_of(i * TILE, TILE), TILE)
            got = dot(rows_m[part, :], vcat[b])
            mask = lane_m[part, :]
            picked[part, 0:LANES] = (got[:, 0:LANES] * mask).astype(bf16)
            picked[part, LANES:] = (got[:, LANES:] * mask).astype(bf16)

        both = dot(m_row[...], picked[...])
        both = both[0:LANES] + both[LANES:]
        both = (both[:, 0:LANES] + both[:, LANES:]).T
        coef_out[app, b] = jnp.sum(both.reshape(LANES // 8, 8, LANES), axis=0)
        for d in range(len(COEF_STEPS)):
            coef_copy(app, b, d).start()

    lane8 = lax.broadcasted_iota(jnp.int32, (8, LANES), 1)
    slot8 = jnp.bitwise_and(lax.shift_right_logical(lane8, 3), 3)

    def near_total(app, b):
        total = coef_out[app, b]
        for d, step in enumerate(COEF_STEPS):
            coef_copy(app, b, d).wait_recv()
            shift = -step
            there = grid + shift
            lands = slot8 + shift
            keep = (slot8 < 3) & (lands >= 0) & (lands < 3) & (there >= 0) & (there < n_grid)
            total = total + pltpu.roll(
                jnp.where(keep, coef_in[app, b, d], 0.0), (8 * shift) % LANES, 1
            )
        return jnp.broadcast_to(jnp.sum(total, axis=0, keepdims=True), (8, LANES))

    def coupling_rows():
        total = cp_ref[...]
        for k, step in enumerate((-1, 1)):
            shift = -step
            there = grid + shift
            keep = (there >= 0) & (there < n_grid)
            total = total + pltpu.roll(
                jnp.where(keep, coup_in[k], 0.0), (8 * shift) % LANES, 1
            )
        return total

    def inner_terms(ext, b, app):
        near_c = near_total(app, b)
        mix = coupling_rows()
        mixed = jnp.zeros((8, LANES), f32)
        for k in range(4):
            turned = near_c if k == 0 else pltpu.roll(near_c, LANES - GROUP * k, 1)
            mixed = mixed + jnp.broadcast_to(mix[k : k + 1], (8, LANES)) * turned
        high, low = split(jnp.broadcast_to(mixed[0:1] * (1.0 / HALF), (LANES, LANES)))
        wcat[0:LANES, 0:LANES] = high
        wcat[0:LANES, LANES:] = high
        wcat[LANES:, 0:LANES] = low
        wcat[LANES:, LANES:] = jnp.zeros((LANES, LANES), bf16)

        @pl.loop(0, ent // TILE)
        def _(i):
            part = pl.ds(pl.multiple_of(i * TILE, TILE), TILE)
            back = lax.dot_general(
                m_col[part, :], wcat[...], (((1,), (1,)), ((), ())), preferred_element_type=f32
            )
            high, low = split((back[:, 0:LANES] + back[:, LANES:]) * lane_m[part, :])
            spread[part, 0:LANES] = high
            spread[part, LANES:] = low

        step = 2 * ny

        @pl.loop(0, plane_rows // step)
        def _(i):
            part = pl.ds(pl.multiple_of(i * step, step), step)
            both = dot(rows_t[part, :], spread[...]) + dot(vcat[b, part, :], zmat[...])
            acc[part, :] = both[:, 0:LANES] + both[:, LANES:]

        row = lax.broadcasted_iota(jnp.int32, (ny, LANES), 0)

        @pl.loop(0, nx)
        def _(x):
            first = pl.multiple_of(x * ny, ny)
            cells = ext[b, pl.ds(pl.multiple_of(reach_rows + first, ny), ny), :]
            total = acc[pl.ds(first, ny), :]
            for k in range(1, REACH + 1):
                before = jnp.where(row >= k, pltpu.roll(cells, k, 0), 0.0)
                after = jnp.where(row < ny - k, pltpu.roll(cells, ny - k, 0), 0.0)
                total = total + EK[k - 1] * (before + after)
            acc[pl.ds(first, ny), :] = total

    def along_x(ext, b, store):
        @pl.loop(0, ny // 8)
        def _(t):
            first = pl.multiple_of(t * 8, 8)
            cells = [
                ext[b, pl.ds(pl.multiple_of(x * ny + first, 8), 8), :]
                for x in range(nx + 2 * REACH)
            ]
            for x in range(nx):
                place = pl.ds(pl.multiple_of(x * ny + first, 8), 8)
                here = cells[x + REACH]
                total = acc[place, :] + here * (pot_ref[place, :] * (1.0 / HALF) + DIAG)
                for k in range(1, REACH + 1):
                    total = total + EK[k - 1] * (cells[x + REACH + k] + cells[x + REACH - k])
                store(x, first, place, total)

    @pl.loop(0, norb)
    def _(b):
        own_copy(b).wait()
        coefficients(ext1, b, 0)

    for k in range(2):
        coup_copy(k).wait_recv()

    @pl.loop(0, norb)
    def _(b):
        inner_terms(ext1, b, 0)
        wait_halos(b, 0, False)

        def store(x, first, place, total):
            ext2[b, pl.ds(pl.multiple_of(reach_rows + x * ny + first, 8), 8), :] = total

        along_x(ext1, b, store)
        send_halos(b, 1)
        coefficients(ext2, b, 1)

    def scatter_copy(b, to):
        part = pl.ds(pl.multiple_of(to * piece, 8), piece)
        return pltpu.make_async_remote_copy(
            src_ref=filt.at[b, part], dst_ref=panel.at[b, part],
            send_sem=scat_send.at[b, to], recv_sem=scat_recv.at[b],
            device_id=(2 * to, grid), device_id_type=MESH,
        )

    def gather_copy(b, step):
        part = pl.ds(pl.multiple_of(chip * piece, 8), piece)
        return pltpu.make_async_remote_copy(
            src_ref=panel.at[b, part], dst_ref=panel.at[b, part],
            send_sem=gath_send.at[b, step], recv_sem=gath_recv.at[b],
            device_id=(other_chip(step), grid), device_id_type=MESH,
        )

    def sibling_copy(b):
        return pltpu.make_async_remote_copy(
            src_ref=panel.at[b], dst_ref=panel.at[b],
            send_sem=sib_send.at[b], recv_sem=sib_recv.at[b],
            device_id=(sibling, grid), device_id_type=MESH,
        )

    def self_copy(b):
        return pltpu.make_async_copy(filt.at[b], panel.at[b], copy_sem.at[b])

    root = band == 0
    follower = main & jnp.logical_not(root)

    def phase_scatter(b):
        @pl.when(root)
        def _():
            @pl.loop(1, chips)
            def _(to):
                scatter_copy(b, to).start()

            self_copy(b).start()

    def phase_gather(b):
        @pl.when(root)
        def _():
            self_copy(b).wait()

        @pl.when(follower)
        def _():
            scatter_copy(b, chip).wait_recv()

        @pl.when(main)
        def _():
            @pl.loop(1, chips)
            def _(step):
                @pl.when(other_chip(step) != 0)
                def _():
                    gather_copy(b, step).start()

    def phase_sibling(b):
        @pl.when(follower)
        def _():
            most = panel.at[b, pl.ds(0, (chips - 1) * piece)]
            pltpu.make_async_copy(most, most, gath_recv.at[b]).wait()

        @pl.when(main)
        def _():
            sibling_copy(b).start()

    def phase_last(b):
        @pl.when(core == 1)
        def _():
            sibling_copy(b).wait_recv()

    @pl.loop(0, norb)
    def _(b):
        inner_terms(ext2, b, 1)
        wait_halos(b, 1, False)

        def store(x, first, place, total):
            before = ext1[b, pl.ds(pl.multiple_of(reach_rows + x * ny + first, 8), 8), :]
            filt[b, place, :] = 2.0 * total - before

        along_x(ext2, b, store)
        phase_scatter(b)

        @pl.when(b >= 1)
        def _():
            phase_gather(b - 1)

        @pl.when(b >= 2)
        def _():
            phase_sibling(b - 2)

    phase_gather(norb - 1)
    phase_sibling(norb - 2)
    phase_sibling(norb - 1)
    for b in range(norb):
        phase_last(b)

    couples = [(k, m) for k in range(norb) for m in range(k + 1)]
    n_pairs = len(couples) + norb * norb

    def add_pairs(t, sums):
        place = pl.ds(pl.multiple_of(t * 8, 8), 8)
        p = [panel[k, place, :] for k in range(norb)]
        f = [filt[n, place, :] for n in range(norb)]
        terms = [p[k] * p[m] for k, m in couples] + [p[k] * f[n] for k in range(norb) for n in range(norb)]
        return tuple(s + term for s, term in zip(sums, terms))

    sums = lax.fori_loop(
        0, plane_rows // 8, add_pairs, tuple(jnp.zeros((8, LANES), f32) for _ in range(n_pairs))
    )
    pairs[...] = jnp.zeros(pairs.shape, f32)
    for i, s in enumerate(sums):
        pairs[i : i + 1, :] = jnp.sum(s, axis=0, keepdims=True)
    gram_out[...] = jnp.sum(pairs[...].T.reshape(LANES // 8, 8, LANES), axis=0)

    def gram_copy(step):
        return pltpu.make_async_remote_copy(
            src_ref=gram_out, dst_ref=gram_in.at[step],
            send_sem=gram_send.at[step], recv_sem=gram_recv.at[step],
            device_id=(band, peer(step)), device_id_type=MESH,
        )

    for step in range(1, n_grid):
        gram_copy(step).start()
    total = gram_out[...]
    for step in range(1, n_grid):
        gram_copy(step).wait_recv()
        total = total + gram_in[step]
    total = jnp.sum(total, axis=0, keepdims=True) * (1.0 / (plane_rows * LANES * n_grid))
    lane1 = lax.broadcasted_iota(jnp.int32, (1, LANES), 1)

    def number(i):
        one = jnp.sum(jnp.where(lane1 == i, total, 0.0), axis=1, keepdims=True)
        return jnp.broadcast_to(one, (8, LANES))

    gram = {couple: number(i) for i, couple in enumerate(couples)}
    raw = [[number(len(couples) + k * norb + n) for n in range(norb)] for k in range(norb)]
    lower, inverse = {}, {}
    for j in range(norb):
        left = gram[j, j]
        for m in range(j):
            left = left - lower[j, m] * lower[j, m]
        lower[j, j] = jnp.sqrt(left)
        inverse[j, j] = 1.0 / lower[j, j]
        for i in range(j + 1, norb):
            left = gram[i, j]
            for m in range(j):
                left = left - lower[i, m] * lower[j, m]
            lower[i, j] = left * inverse[j, j]
    for j in range(norb):
        for i in range(j + 1, norb):
            left = lower[i, j] * inverse[j, j]
            for m in range(j + 1, i):
                left = left + lower[i, m] * inverse[m, j]
            inverse[i, j] = -left * inverse[i, i]
    corr = [
        [sum(inverse[k, m] * raw[m][n] for m in range(k + 1)) for n in range(norb)]
        for k in range(norb)
    ]
    weight = [[None] * norb for _ in range(norb)]
    zero8 = jnp.zeros((8, LANES), f32)
    for m in range(norb):
        for n in range(norb):
            away = -sum(inverse[k, m] * corr[k][n] for k in range(m, norb))
            weight[m][n] = jnp.where(root, inverse[n, m] if m <= n else zero8, away)
    keep = jnp.where(root, zero8, jnp.ones((8, LANES), f32))

    @pl.loop(0, plane_rows // 8)
    def _(t):
        place = pl.ds(pl.multiple_of(t * 8, 8), 8)
        p = [panel[k, place, :] for k in range(norb)]
        for n in range(norb):
            value = keep * filt[n, place, :]
            for m in range(norb):
                value = value + weight[m][n] * p[m]
            out_ref[n, place, :] = value

    @pl.loop(0, norb)
    def _(b):
        wait_halos(b, 0, True)
        wait_halos(b, 1, True)
        for app in range(2):
            for d in range(len(COEF_STEPS)):
                coef_copy(app, b, d).wait_send()

        @pl.when(root)
        def _():
            @pl.loop(1, chips)
            def _(to):
                scatter_copy(b, to).wait_send()

        @pl.when(main)
        def _():
            @pl.loop(1, chips)
            def _(step):
                @pl.when(other_chip(step) != 0)
                def _():
                    gather_copy(b, step).wait_send()

            sibling_copy(b).wait_send()

    for k in range(2):
        coup_copy(k).wait_send()
    for step in range(1, n_grid):
        gram_copy(step).wait_send()


def local(n_band, n_grid, orbitals, potential, projectors, coupling, entry_cell, entry_atom):
    norb, nx, ny, nz = orbitals.shape
    ent = entry_cell.shape[0]
    rows = nx * ny
    chips = n_band // 2
    f32, bf16 = jnp.float32, jnp.bfloat16
    turned = jnp.stack(
        [
            jnp.stack([coupling[:, i, (i + k) % 4] for i in range(4)], axis=0)
            for k in range(4)
        ],
        axis=0,
    )
    mix = jnp.pad(turned, ((0, 4), (0, 0), (ATOM_DEV, GROUP - 2 * ATOM_DEV))).reshape(8, LANES)
    vmem, dma = pltpu.VMEM, pltpu.SemaphoreType.DMA
    ext_rows = rows + 2 * REACH * ny
    whole = pl.BlockSpec(memory_space=pltpu.VMEM)
    out = pl.pallas_call(
        functools.partial(kernel, n_band, n_grid, nx, ny, ent),
        out_shape=jax.ShapeDtypeStruct((norb, rows, nz), f32),
        in_specs=[pl.BlockSpec(memory_space=pl.ANY)] + [whole] * 5,
        out_specs=whole,
        scratch_shapes=[
            vmem((norb, ext_rows, nz), f32),
            vmem((norb, ext_rows, nz), f32),
            vmem((norb, rows, nz), f32),
            vmem((norb, rows, nz), f32),
            vmem((ent, rows), bf16),
            vmem((rows, ent), bf16),
            vmem((ent, LANES), f32),
            vmem((2 * LANES, ent), bf16),
            vmem((ent, 2 * LANES), bf16),
            vmem((ent, 2 * LANES), bf16),
            vmem((ent, 2 * LANES), bf16),
            vmem((norb, rows, 2 * LANES), bf16),
            vmem((rows, LANES), f32),
            vmem((2 * LANES, 2 * LANES), bf16),
            vmem((2 * LANES, 2 * LANES), bf16),
            vmem((ent, 8), f32),
            vmem((2, norb, 8, LANES), f32),
            vmem((2, norb, 4, 8, LANES), f32),
            vmem((2, 8, LANES), f32),
            vmem((LANES, LANES), f32),
            vmem((8, LANES), f32),
            vmem((n_grid, 8, LANES), f32),
            dma((norb,)),
            dma((2, norb, 2)), dma((2, norb, 2)),
            dma((2, norb, 4)), dma((2, norb, 4)),
            dma((2,)), dma((2,)),
            dma((norb, chips)), dma((norb,)),
            dma((norb, chips)), dma((norb,)),
            dma((norb,)), dma((norb,)),
            dma((norb,)),
            dma((n_grid,)), dma((n_grid,)),
        ],
        compiler_params=pltpu.CompilerParams(
            collective_id=0, has_side_effects=True, vmem_limit_bytes=48 * 1024 * 1024
        ),
        name="filter_panel",
    )(
        orbitals.reshape(norb, rows, nz),
        potential.reshape(rows, nz),
        projectors,
        mix,
        entry_cell.reshape(1, ent),
        entry_atom.reshape(1, ent),
    )
    return out.reshape(orbitals.shape)


def solution(mesh):
    return jax.shard_map(
        functools.partial(local, mesh.shape["band"], mesh.shape["grid"]),
        mesh=mesh,
        in_specs=(
            P("band", "grid", None, None),
            P("grid", None, None),
            P(None, "grid"),
            P("grid", None, None),
            P("grid"),
            P("grid"),
        ),
        out_specs=P("band", "grid", None, None),
        check_vma=False,
    )
```

time: 696 us -> 115 us (0.17)
  the two profiles are of different devices: /device:TPU:32 before, /device:TPU:9 now
where the time goes in v1:
time: 115 us
  Pallas kernels  108 us (94%)
  local copies, waits for them, and re-layouts  6.46 us (6%)
    pallas_call x1, Pallas kernels, local(): pl.pallas_call(functools.partial(kernel, n_band, n_grid, nx, ny, ent), ou...  108 us
    unnamed x11, local copies, waits for them, and re-layouts  5.5 us

profile of v1, /device:TPU:9, one launch (start us, length us, event | category | flops | bytes accessed | tf_op | source)
XLA Modules:
  0.0 114.7 jit_solution(5312835572251867714)
XLA Ops:
  0.0 0.9 slice_bitcast_fusion.15
  0.9 0.1 select_maximum_fusion
  1.0 0.1 reshape.20.cp_ref
  1.1 0.0 copy-start
  1.1 1.3 %copy-done = f32[4,8,80,128]{3,2,1,0:T(8,128)S(1)} copy-done((f32[4,8,80,128]{3,2,1,0:T(8,128)S(1)}, f32[4,8,80,128]{3,2,1,0:T(8,128)}, u32[]{:S(2)}) %copy-start) | copy-done | bytes 1310744
  2.4 0.0 copy-start.1
  2.4 1.0 copy-done.1
  3.4 0.0 copy-start.2
  3.4 0.8 copy-done.2
  4.1 0.0 copy-start.3
  4.1 0.7 copy-done.3
  4.8 0.0 copy-start.4
  4.8 0.7 copy-done.4
  5.5 108.1 %filter_panel.1 = f32[4,640,128]{2,1,0:T(8,128)S(1)} custom-call(f32[4,640,128]{2,1,0:T(8,128)S(1)} %bitcast.46, f32[640,128]{1,0:T(8,128)S(1)} %bitcast.47, f32[4,2048]{1,0:T(4,128)S(1)} %copy-done.2, f32[8,128]{1,0:T(8,128)S(1)} %reshape.20.cp_ref, s32[1,2048]{1,0:T(1,128)S(1)} %bitcast.48, s32[1,2048]{1,0:T(1,128)S(1)} %bitcast.49), custom_call_target="tpu_custom_call" | custom-call | tf_op jit(solution)/shard_map/filter_panel/pallas_call | solution.py:580
  113.6 1.1 copy.8
  (2 shorter events, 0.0 us)
Async XLA Ops:
  1.1 1.3 %copy-start = (f32[4,8,80,128]{3,2,1,0:T(8,128)S(1)}, f32[4,8,80,128]{3,2,1,0:T(8,128)}, u32[]{:S(2)}) copy-start(f32[4,8,80,128]{3,2,1,0:T(8,128)} %param.6) | copy-start | bytes 3932164
  2.4 1.0 copy-start.1
  3.4 0.8 copy-start.2
  4.1 0.7 copy-start.3
  4.8 0.7 copy-start.4

commit v2 on v1

--- a/solution.py
+++ b/solution.py
@@ -16,6 +16,7 @@
 ATOM_DEV = 8
 GROUP = 32
 TILE = 256
+WIDE = 512
 MESH = pl.DeviceIdType.MESH
 COEF_STEPS = (-2, -1, 1, 2)
 
@@ -46,12 +47,13 @@
 
 def kernel(
     n_band, n_grid, nx, ny, ent,
-    orb_ref, pot_ref, proj_ref, cp_ref, cell_ref, atom_ref,
+    orb_ref, pot_hbm, proj_hbm, coup_hbm, cell_hbm, atom_hbm,
     out_ref,
+    pot_ref, proj_ref, coup_ref, cell_ref, atom_ref,
     ext1, ext2, filt, panel, rows_m, rows_t, lane_m, m_row, m_col, picked, spread, vcat, acc,
-    zmat, wcat, cols, coef_out, coef_in, coup_in, pairs, gram_out, gram_in,
-    own_sem, halo_send, halo_recv, coef_send, coef_recv, coup_send, coup_recv,
-    scat_send, scat_recv, gath_send, gath_recv, sib_send, sib_recv, copy_sem,
+    zmat, wcat, cols, coef_out, coef_in, coup_own, coup_in, mix, pairs, gram_out, gram_in,
+    load_sem, own_sem, halo_send, halo_recv, coef_send, coef_recv, coup_send, coup_recv,
+    scat_send, scat_recv, z_send, z_recv, y_send, y_recv, sib_send, sib_recv, copy_sem,
     gram_send, gram_recv,
 ):
     f32, bf16 = jnp.float32, jnp.bfloat16
@@ -59,9 +61,13 @@
     plane_rows = nx * ny
     reach_rows = REACH * ny
     chips = n_band // 2
+    n_zh = 4 if chips % 4 == 0 else 1
+    n_y = chips // n_zh
     piece = plane_rows // chips
+    share = piece * n_zh
     band, grid = lax.axis_index("band"), lax.axis_index("grid")
     chip = lax.div(band, 2)
+    zh, yy = lax.rem(chip, n_zh), lax.div(chip, n_zh)
     core = lax.rem(band, 2)
     sibling = band + 1 - 2 * core
     main = core == 0
@@ -70,23 +76,65 @@
     def peer(step):
         return lax.rem(grid + step + n_grid, n_grid)
 
+    loads = [
+        pltpu.make_async_copy(source, there, load_sem.at[i])
+        for i, (source, there) in enumerate(
+            [
+                (cell_hbm, cell_ref), (atom_hbm, atom_ref), (proj_hbm, proj_ref),
+                (coup_hbm, coup_ref), (pot_hbm, pot_ref),
+            ]
+        )
+    ]
+    for load in loads:
+        load.start()
+
     barrier = pltpu.get_barrier_semaphore()
     for step in range(1, n_grid):
         pl.semaphore_signal(barrier, inc=1, device_id=(band, peer(step)), device_id_type=MESH)
     pl.semaphore_signal(barrier, inc=1, device_id=(sibling, grid), device_id_type=MESH)
 
-    def other_chip(step):
-        return 2 * lax.rem(chip + step, chips)
+    def along_z(step):
+        return 2 * (yy * n_zh + lax.rem(zh + step, n_zh))
+
+    def along_y(step):
+        return 2 * (lax.rem(yy + step, n_y) * n_zh + zh)
+
+    root = band == 0
+    follower = main & jnp.logical_not(root)
+    crossed = (zh > 0) & (yy > 0)
 
     @pl.when(main)
     def _():
-        @pl.loop(1, chips)
-        def _(step):
+        for step in range(1, n_zh):
             pl.semaphore_signal(
-                barrier, inc=1, device_id=(other_chip(step), grid), device_id_type=MESH
+                barrier, inc=1, device_id=(along_z(step), grid), device_id_type=MESH
             )
-
-        pl.semaphore_wait(barrier, n_grid + chips - 1)
+        for step in range(1, n_y):
+            pl.semaphore_signal(
+                barrier, inc=1, device_id=(along_y(step), grid), device_id_type=MESH
+            )
+
+        @pl.when(crossed)
+        def _():
+            pl.semaphore_signal(barrier, inc=1, device_id=(0, grid), device_id_type=MESH)
+
+        @pl.when(root)
+        def _():
+            for y in range(1, n_y):
+                for z in range(1, n_zh):
+                    pl.semaphore_signal(
+                        barrier, inc=1, device_id=(2 * (y * n_zh + z), grid), device_id_type=MESH
+                    )
+
+            pl.semaphore_wait(barrier, n_grid + chips - 1)
+
+        @pl.when(crossed)
+        def _():
+            pl.semaphore_wait(barrier, n_grid + n_zh + n_y - 1)
+
+        @pl.when(jnp.logical_not(crossed | root))
+        def _():
+            pl.semaphore_wait(barrier, n_grid + n_zh + n_y - 2)
 
     @pl.when(core == 1)
     def _():
@@ -146,9 +194,16 @@
         send_halos(b, 0)
         own_copy(b).start()
 
+    for load in loads[:4]:
+        load.wait()
+    coup_own[...] = jnp.zeros(coup_own.shape, f32)
+    for i in range(4):
+        first = GROUP * i + ATOM_DEV
+        coup_own[0:4, first : first + ATOM_DEV] = coup_ref[i]
+
     def coup_copy(k):
         return pltpu.make_async_remote_copy(
-            src_ref=cp_ref, dst_ref=coup_in.at[k],
+            src_ref=coup_own, dst_ref=coup_in.at[k],
             send_sem=coup_send.at[k], recv_sem=coup_recv.at[k],
             device_id=(band, peer((-1, 1)[k])), device_id_type=MESH,
         )
@@ -189,7 +244,7 @@
         lane = lax.broadcasted_iota(jnp.int32, (TILE, LANES), 1).astype(f32)
         wide = lax.broadcasted_iota(jnp.int32, (TILE, plane_rows), 1).astype(f32)
         rows_m[part, :] = jnp.where(column[:, 0:1] == wide, 1.0, 0.0).astype(bf16)
-        lane_m[part, :] = jnp.where(column[:, 1:2] == lane, 1.0, 0.0)
+        lane_m[part, :] = jnp.where(column[:, 1:2] == lane, 1.0, 0.0).astype(bf16)
         total = jnp.zeros((TILE, LANES), f32)
         for j in range(4):
             total = jnp.where(column[:, 2:3] + (GROUP * j) == lane, column[:, 4 + j : 5 + j], total)
@@ -232,13 +287,11 @@
     def coefficients(ext, b, app):
         cut(ext, b)
 
-        @pl.loop(0, ent // TILE)
-        def _(i):
-            part = pl.ds(pl.multiple_of(i * TILE, TILE), TILE)
-            got = dot(rows_m[part, :], vcat[b])
-            mask = lane_m[part, :]
-            picked[part, 0:LANES] = (got[:, 0:LANES] * mask).astype(bf16)
-            picked[part, LANES:] = (got[:, LANES:] * mask).astype(bf16)
+        for i in range(0, ent, WIDE):
+            got = dot(rows_m[i : i + WIDE, :], vcat[b]).astype(bf16)
+            mask = lane_m[i : i + WIDE, :]
+            picked[i : i + WIDE, 0:LANES] = got[:, 0:LANES] * mask
+            picked[i : i + WIDE, LANES:] = got[:, LANES:] * mask
 
         both = dot(m_row[...], picked[...])
         both = both[0:LANES] + both[LANES:]
@@ -264,44 +317,45 @@
         return jnp.broadcast_to(jnp.sum(total, axis=0, keepdims=True), (8, LANES))
 
     def coupling_rows():
-        total = cp_ref[...]
+        total = coup_own[...]
         for k, step in enumerate((-1, 1)):
+            coup_copy(k).wait_recv()
             shift = -step
             there = grid + shift
             keep = (there >= 0) & (there < n_grid)
             total = total + pltpu.roll(
                 jnp.where(keep, coup_in[k], 0.0), (8 * shift) % LANES, 1
             )
-        return total
+        group = lax.shift_right_logical(lax.broadcasted_iota(jnp.int32, (1, LANES), 1), 5)
+        for k in range(4):
+            line = jnp.zeros((1, LANES), f32)
+            for i in range(4):
+                j = (i + k) % 4
+                line = jnp.where(group == i, total[j : j + 1], line)
+            mix[8 * k : 8 * k + 8, :] = jnp.broadcast_to(line * (1.0 / HALF), (8, LANES))
 
     def inner_terms(ext, b, app):
         near_c = near_total(app, b)
-        mix = coupling_rows()
-        mixed = jnp.zeros((8, LANES), f32)
-        for k in range(4):
-            turned = near_c if k == 0 else pltpu.roll(near_c, LANES - GROUP * k, 1)
-            mixed = mixed + jnp.broadcast_to(mix[k : k + 1], (8, LANES)) * turned
-        high, low = split(jnp.broadcast_to(mixed[0:1] * (1.0 / HALF), (LANES, LANES)))
+        mixed = mix[0:8, :] * near_c
+        for k in range(1, 4):
+            mixed = mixed + mix[8 * k : 8 * k + 8, :] * pltpu.roll(near_c, LANES - GROUP * k, 1)
+        high, low = split(jnp.broadcast_to(mixed[0:1], (LANES, LANES)).T)
         wcat[0:LANES, 0:LANES] = high
-        wcat[0:LANES, LANES:] = high
-        wcat[LANES:, 0:LANES] = low
+        wcat[0:LANES, LANES:] = low
+        wcat[LANES:, 0:LANES] = high
         wcat[LANES:, LANES:] = jnp.zeros((LANES, LANES), bf16)
 
-        @pl.loop(0, ent // TILE)
-        def _(i):
-            part = pl.ds(pl.multiple_of(i * TILE, TILE), TILE)
-            back = lax.dot_general(
-                m_col[part, :], wcat[...], (((1,), (1,)), ((), ())), preferred_element_type=f32
-            )
-            high, low = split((back[:, 0:LANES] + back[:, LANES:]) * lane_m[part, :])
-            spread[part, 0:LANES] = high
-            spread[part, LANES:] = low
-
-        step = 2 * ny
-
-        @pl.loop(0, plane_rows // step)
-        def _(i):
-            part = pl.ds(pl.multiple_of(i * step, step), step)
+        for i in range(0, ent, WIDE):
+            back = dot(m_col[i : i + WIDE, :], wcat[...])
+            high, low = split(back[:, 0:LANES] + back[:, LANES:])
+            mask = lane_m[i : i + WIDE, :]
+            spread[i : i + WIDE, 0:LANES] = high * mask
+            spread[i : i + WIDE, LANES:] = low * mask
+
+        step = 4 * ny
+
+        for i in range(0, plane_rows, step):
+            part = slice(i, i + step)
             both = dot(rows_t[part, :], spread[...]) + dot(vcat[b, part, :], zmat[...])
             acc[part, :] = both[:, 0:LANES] + both[:, LANES:]
 
@@ -339,8 +393,8 @@
         own_copy(b).wait()
         coefficients(ext1, b, 0)
 
-    for k in range(2):
-        coup_copy(k).wait_recv()
+    coupling_rows()
+    loads[4].wait()
 
     @pl.loop(0, norb)
     def _(b):
@@ -362,12 +416,20 @@
             device_id=(2 * to, grid), device_id_type=MESH,
         )
 
-    def gather_copy(b, step):
+    def z_copy(b, step):
         part = pl.ds(pl.multiple_of(chip * piece, 8), piece)
         return pltpu.make_async_remote_copy(
             src_ref=panel.at[b, part], dst_ref=panel.at[b, part],
-            send_sem=gath_send.at[b, step], recv_sem=gath_recv.at[b],
-            device_id=(other_chip(step), grid), device_id_type=MESH,
+            send_sem=z_send.at[b, step], recv_sem=z_recv.at[b],
+            device_id=(along_z(step), grid), device_id_type=MESH,
+        )
+
+    def y_copy(b, step):
+        part = pl.ds(pl.multiple_of(yy * share, 8), share)
+        return pltpu.make_async_remote_copy(
+            src_ref=panel.at[b, part], dst_ref=panel.at[b, part],
+            send_sem=y_send.at[b, step], recv_sem=y_recv.at[b],
+            device_id=(along_y(step), grid), device_id_type=MESH,
         )
 
     def sibling_copy(b):
@@ -380,9 +442,6 @@
     def self_copy(b):
         return pltpu.make_async_copy(filt.at[b], panel.at[b], copy_sem.at[b])
 
-    root = band == 0
-    follower = main & jnp.logical_not(root)
-
     def phase_scatter(b):
         @pl.when(root)
         def _():
@@ -392,7 +451,7 @@
 
             self_copy(b).start()
 
-    def phase_gather(b):
+    def phase_z(b):
         @pl.when(root)
         def _():
             self_copy(b).wait()
@@ -403,17 +462,31 @@
 
         @pl.when(main)
         def _():
-            @pl.loop(1, chips)
-            def _(step):
-                @pl.when(other_chip(step) != 0)
+            for step in range(1, n_zh):
+                @pl.when(along_z(step) != 0)
                 def _():
-                    gather_copy(b, step).start()
+                    z_copy(b, step).start()
+
+    def phase_y(b):
+        if n_zh > 1:
+            @pl.when(follower)
+            def _():
+                most = panel.at[b, pl.ds(0, share - piece)]
+                pltpu.make_async_copy(most, most, z_recv.at[b]).wait()
+
+        @pl.when(main)
+        def _():
+            for step in range(1, n_y):
+                @pl.when(along_y(step) != 0)
+                def _():
+                    y_copy(b, step).start()
 
     def phase_sibling(b):
-        @pl.when(follower)
-        def _():
-            most = panel.at[b, pl.ds(0, (chips - 1) * piece)]
-            pltpu.make_async_copy(most, most, gath_recv.at[b]).wait()
+        if n_y > 1:
+            @pl.when(follower)
+            def _():
+                most = panel.at[b, pl.ds(0, plane_rows - share)]
+                pltpu.make_async_copy(most, most, y_recv.at[b]).wait()
 
         @pl.when(main)
         def _():
@@ -438,13 +511,20 @@
 
         @pl.when(b >= 1)
         def _():
-            phase_gather(b - 1)
+            phase_z(b - 1)
 
         @pl.when(b >= 2)
         def _():
-            phase_sibling(b - 2)
-
-    phase_gather(norb - 1)
+            phase_y(b - 2)
+
+        @pl.when(b >= 3)
+        def _():
+            phase_sibling(b - 3)
+
+    phase_z(norb - 1)
+    phase_y(norb - 2)
+    phase_sibling(norb - 3)
+    phase_y(norb - 1)
     phase_sibling(norb - 2)
     phase_sibling(norb - 1)
     for b in range(norb):
@@ -546,11 +626,15 @@
 
         @pl.when(main)
         def _():
-            @pl.loop(1, chips)
-            def _(step):
-                @pl.when(other_chip(step) != 0)
+            for step in range(1, n_zh):
+                @pl.when(along_z(step) != 0)
                 def _():
-                    gather_copy(b, step).wait_send()
+                    z_copy(b, step).wait_send()
+
+            for step in range(1, n_y):
+                @pl.when(along_y(step) != 0)
+                def _():
+                    y_copy(b, step).wait_send()
 
             sibling_copy(b).wait_send()
 
@@ -566,30 +650,27 @@
     rows = nx * ny
     chips = n_band // 2
     f32, bf16 = jnp.float32, jnp.bfloat16
-    turned = jnp.stack(
-        [
-            jnp.stack([coupling[:, i, (i + k) % 4] for i in range(4)], axis=0)
-            for k in range(4)
-        ],
-        axis=0,
-    )
-    mix = jnp.pad(turned, ((0, 4), (0, 0), (ATOM_DEV, GROUP - 2 * ATOM_DEV))).reshape(8, LANES)
     vmem, dma = pltpu.VMEM, pltpu.SemaphoreType.DMA
     ext_rows = rows + 2 * REACH * ny
     whole = pl.BlockSpec(memory_space=pltpu.VMEM)
     out = pl.pallas_call(
         functools.partial(kernel, n_band, n_grid, nx, ny, ent),
         out_shape=jax.ShapeDtypeStruct((norb, rows, nz), f32),
-        in_specs=[pl.BlockSpec(memory_space=pl.ANY)] + [whole] * 5,
+        in_specs=[pl.BlockSpec(memory_space=pltpu.HBM)] * 6,
         out_specs=whole,
         scratch_shapes=[
+            vmem((rows, nz), f32),
+            vmem(projectors.shape, f32),
+            vmem((4, 4, ATOM_DEV), f32),
+            vmem((1, ent), jnp.int32),
+            vmem((1, ent), jnp.int32),
             vmem((norb, ext_rows, nz), f32),
             vmem((norb, ext_rows, nz), f32),
             vmem((norb, rows, nz), f32),
             vmem((norb, rows, nz), f32),
             vmem((ent, rows), bf16),
             vmem((rows, ent), bf16),
-            vmem((ent, LANES), f32),
+            vmem((ent, LANES), bf16),
             vmem((2 * LANES, ent), bf16),
             vmem((ent, 2 * LANES), bf16),
             vmem((ent, 2 * LANES), bf16),
@@ -601,29 +682,33 @@
             vmem((ent, 8), f32),
             vmem((2, norb, 8, LANES), f32),
             vmem((2, norb, 4, 8, LANES), f32),
+            vmem((8, LANES), f32),
             vmem((2, 8, LANES), f32),
+            vmem((32, LANES), f32),
             vmem((LANES, LANES), f32),
             vmem((8, LANES), f32),
             vmem((n_grid, 8, LANES), f32),
+            dma((5,)),
             dma((norb,)),
             dma((2, norb, 2)), dma((2, norb, 2)),
             dma((2, norb, 4)), dma((2, norb, 4)),
             dma((2,)), dma((2,)),
             dma((norb, chips)), dma((norb,)),
-            dma((norb, chips)), dma((norb,)),
+            dma((norb, 4)), dma((norb,)),
+            dma((norb, 16)), dma((norb,)),
             dma((norb,)), dma((norb,)),
             dma((norb,)),
             dma((n_grid,)), dma((n_grid,)),
         ],
         compiler_params=pltpu.CompilerParams(
-            collective_id=0, has_side_effects=True, vmem_limit_bytes=48 * 1024 * 1024
+            collective_id=0, has_side_effects=True, vmem_limit_bytes=62 * 1024 * 1024
         ),
         name="filter_panel",
     )(
         orbitals.reshape(norb, rows, nz),
         potential.reshape(rows, nz),
         projectors,
-        mix,
+        coupling.transpose(1, 2, 0),
         entry_cell.reshape(1, ent),
         entry_atom.reshape(1, ent),
     )

time: 115 us -> 93.6 us (0.81)
  the two profiles are of different devices: /device:TPU:9 before, /device:TPU:65 now
where the time goes in v2:
time: 93.6 us; the launch traced here: 93.5 us
  Pallas kernels  91 us (97%)
  local copies, waits for them, and re-layouts  2.5 us (3%)
    pallas_call x1, Pallas kernels, local(): pl.pallas_call(functools.partial(kernel, n_band, n_grid, nx, ny, ent), ou...  91 us
    unnamed x1, local copies, waits for them, and re-layouts  2.5 us

profile of v2, /device:TPU:65, one launch (start us, length us, event | category | flops | bytes accessed | tf_op | source)
XLA Modules:
  0.0 93.5 jit_solution(8008654102432950421)
XLA Ops:
  0.0 91.0 %filter_panel.1 = f32[4,640,128]{2,1,0:T(8,128)} custom-call(f32[4,640,128]{2,1,0:T(8,128)} %bitcast.7, f32[640,128]{1,0:T(8,128)} %bitcast.8, f32[4,2048]{1,0:T(4,128)} %proj_hbm.1, f32[4,4,8]{2,1,0:T(4,128)} %bitcast.9, s32[1,2048]{1,0:T(1,128)} %bitcast.10, s32[1,2048]{1,0:T(1,128)} %bitcast.11), custom_call_target="tpu_custom_call" | custom-call | tf_op jit(solution)/shard_map/filter_panel/pallas_call | solution.py:656
  91.0 2.5 %copy.8 = f32[4,8,80,128]{3,2,1,0:T(8,128)} copy(f32[4,8,80,128]{3,2,1,0:T(8,128)} %bitcast.6) | data formatting | bytes 2621440

commit v3 on v2

--- a/solution.py
+++ b/solution.py
@@ -16,6 +16,8 @@
 ATOM_DEV = 8
 GROUP = 32
 TILE = 256
+LAG = 1
+TURN = 2
 WIDE = 512
 MESH = pl.DeviceIdType.MESH
 COEF_STEPS = (-2, -1, 1, 2)
@@ -52,7 +54,7 @@
     pot_ref, proj_ref, coup_ref, cell_ref, atom_ref,
     ext1, ext2, filt, panel, rows_m, rows_t, lane_m, m_row, m_col, picked, spread, vcat, acc,
     zmat, wcat, cols, coef_out, coef_in, coup_own, coup_in, mix, pairs, gram_out, gram_in,
-    load_sem, own_sem, halo_send, halo_recv, coef_send, coef_recv, coup_send, coup_recv,
+    load_sem, turn_sem, own_sem, halo_send, halo_recv, coef_send, coef_recv, coup_send, coup_recv,
     scat_send, scat_recv, z_send, z_recv, y_send, y_recv, sib_send, sib_recv, copy_sem,
     gram_send, gram_recv,
 ):
@@ -63,8 +65,9 @@
     chips = n_band // 2
     n_zh = 4 if chips % 4 == 0 else 1
     n_y = chips // n_zh
-    piece = plane_rows // chips
-    share = piece * n_zh
+    ringed = n_zh > 1
+    share = plane_rows // n_y
+    half = share // 2
     band, grid = lax.axis_index("band"), lax.axis_index("grid")
     chip = lax.div(band, 2)
     zh, yy = lax.rem(chip, n_zh), lax.div(chip, n_zh)
@@ -101,40 +104,17 @@
 
     root = band == 0
     follower = main & jnp.logical_not(root)
-    crossed = (zh > 0) & (yy > 0)
+    greeted = [along_z(step) for step in (1, n_zh - 1)] if ringed else []
+    greeted += [along_y(step) for step in range(1, n_y)]
 
     @pl.when(main)
     def _():
-        for step in range(1, n_zh):
-            pl.semaphore_signal(
-                barrier, inc=1, device_id=(along_z(step), grid), device_id_type=MESH
-            )
-        for step in range(1, n_y):
-            pl.semaphore_signal(
-                barrier, inc=1, device_id=(along_y(step), grid), device_id_type=MESH
-            )
-
-        @pl.when(crossed)
-        def _():
-            pl.semaphore_signal(barrier, inc=1, device_id=(0, grid), device_id_type=MESH)
-
-        @pl.when(root)
-        def _():
-            for y in range(1, n_y):
-                for z in range(1, n_zh):
-                    pl.semaphore_signal(
-                        barrier, inc=1, device_id=(2 * (y * n_zh + z), grid), device_id_type=MESH
-                    )
-
-            pl.semaphore_wait(barrier, n_grid + chips - 1)
-
-        @pl.when(crossed)
-        def _():
-            pl.semaphore_wait(barrier, n_grid + n_zh + n_y - 1)
-
-        @pl.when(jnp.logical_not(crossed | root))
-        def _():
-            pl.semaphore_wait(barrier, n_grid + n_zh + n_y - 2)
+        for to in greeted:
+            pl.semaphore_signal(barrier, inc=1, device_id=(to, grid), device_id_type=MESH)
+
+    @pl.when(follower)
+    def _():
+        pl.semaphore_wait(barrier, n_grid + len(greeted))
 
     @pl.when(core == 1)
     def _():
@@ -189,10 +169,15 @@
             orb_ref.at[b], ext1.at[b, pl.ds(reach_rows, plane_rows)], own_sem.at[b]
         )
 
+    waits_turn = band == 1
+
     @pl.loop(0, norb)
     def _(b):
-        send_halos(b, 0)
         own_copy(b).start()
+
+        @pl.when(band > 1)
+        def _():
+            send_halos(b, 0)
 
     for load in loads[:4]:
         load.wait()
@@ -207,9 +192,6 @@
             send_sem=coup_send.at[k], recv_sem=coup_recv.at[k],
             device_id=(band, peer((-1, 1)[k])), device_id_type=MESH,
         )
-
-    for k in range(2):
-        coup_copy(k).start()
 
     zero_halo = jnp.zeros((norb, reach_rows, LANES), f32)
     for ext in (ext1, ext2):
@@ -245,18 +227,17 @@
         wide = lax.broadcasted_iota(jnp.int32, (TILE, plane_rows), 1).astype(f32)
         rows_m[part, :] = jnp.where(column[:, 0:1] == wide, 1.0, 0.0).astype(bf16)
         lane_m[part, :] = jnp.where(column[:, 1:2] == lane, 1.0, 0.0).astype(bf16)
-        total = jnp.zeros((TILE, LANES), f32)
-        for j in range(4):
-            total = jnp.where(column[:, 2:3] + (GROUP * j) == lane, column[:, 4 + j : 5 + j], total)
-        high, low = split(total)
-        m_col[part, 0:LANES] = high
-        m_col[part, LANES:] = low
-
-    @pl.loop(0, nx)
-    def _(x):
-        first = pl.multiple_of(x * ny, ny)
-        down = lax.broadcasted_iota(jnp.int32, (ny, ent), 0) + first
-        rows_t[pl.ds(first, ny), :] = jnp.where(down == row_of, 1.0, 0.0).astype(bf16)
+
+    @pl.when(root)
+    def _():
+        pl.semaphore_wait(barrier, n_grid + len(greeted))
+
+        @pl.loop(0, norb)
+        def _(b):
+            send_halos(b, 0)
+
+    for k in range(2):
+        coup_copy(k).start()
 
     apart = jnp.abs(
         lax.broadcasted_iota(jnp.int32, (LANES, LANES), 0)
@@ -287,11 +268,24 @@
     def coefficients(ext, b, app):
         cut(ext, b)
 
-        for i in range(0, ent, WIDE):
-            got = dot(rows_m[i : i + WIDE, :], vcat[b]).astype(bf16)
-            mask = lane_m[i : i + WIDE, :]
-            picked[i : i + WIDE, 0:LANES] = got[:, 0:LANES] * mask
-            picked[i : i + WIDE, LANES:] = got[:, LANES:] * mask
+        row = lax.broadcasted_iota(jnp.int32, (ny, LANES), 0)
+        steps = ent // WIDE
+        for i in range(steps):
+            part = slice(i * WIDE, (i + 1) * WIDE)
+            got = dot(rows_m[part, :], vcat[b]).astype(bf16)
+            mask = lane_m[part, :]
+            picked[part, 0:LANES] = got[:, 0:LANES] * mask
+            picked[part, LANES:] = got[:, LANES:] * mask
+            for x in range(i * nx // steps, (i + 1) * nx // steps):
+                place = slice(x * ny, (x + 1) * ny)
+                cells = ext[b, reach_rows + x * ny : reach_rows + (x + 1) * ny, :]
+                both = dot(vcat[b, place, :], zmat[...])
+                total = both[:, 0:LANES] + both[:, LANES:]
+                for k in range(1, REACH + 1):
+                    before = jnp.where(row >= k, pltpu.roll(cells, k, 0), 0.0)
+                    after = jnp.where(row < ny - k, pltpu.roll(cells, ny - k, 0), 0.0)
+                    total = total + EK[k - 1] * (before + after)
+                acc[b, place, :] = total
 
         both = dot(m_row[...], picked[...])
         both = both[0:LANES] + both[LANES:]
@@ -355,22 +349,8 @@
         step = 4 * ny
 
         for i in range(0, plane_rows, step):
-            part = slice(i, i + step)
-            both = dot(rows_t[part, :], spread[...]) + dot(vcat[b, part, :], zmat[...])
-            acc[part, :] = both[:, 0:LANES] + both[:, LANES:]
-
-        row = lax.broadcasted_iota(jnp.int32, (ny, LANES), 0)
-
-        @pl.loop(0, nx)
-        def _(x):
-            first = pl.multiple_of(x * ny, ny)
-            cells = ext[b, pl.ds(pl.multiple_of(reach_rows + first, ny), ny), :]
-            total = acc[pl.ds(first, ny), :]
-            for k in range(1, REACH + 1):
-                before = jnp.where(row >= k, pltpu.roll(cells, k, 0), 0.0)
-                after = jnp.where(row < ny - k, pltpu.roll(cells, ny - k, 0), 0.0)
-                total = total + EK[k - 1] * (before + after)
-            acc[pl.ds(first, ny), :] = total
+            both = dot(rows_t[i : i + step, :], spread[...])
+            acc[b, i : i + step, :] = acc[b, i : i + step, :] + (both[:, 0:LANES] + both[:, LANES:])
 
     def along_x(ext, b, store):
         @pl.loop(0, ny // 8)
@@ -383,7 +363,7 @@
             for x in range(nx):
                 place = pl.ds(pl.multiple_of(x * ny + first, 8), 8)
                 here = cells[x + REACH]
-                total = acc[place, :] + here * (pot_ref[place, :] * (1.0 / HALF) + DIAG)
+                total = acc[b, place, :] + here * (pot_ref[place, :] * (1.0 / HALF) + DIAG)
                 for k in range(1, REACH + 1):
                     total = total + EK[k - 1] * (cells[x + REACH + k] + cells[x + REACH - k])
                 store(x, first, place, total)
@@ -393,6 +373,32 @@
         own_copy(b).wait()
         coefficients(ext1, b, 0)
 
+    @pl.when(waits_turn)
+    def _():
+        pl.semaphore_wait(turn_sem, 1)
+
+        @pl.loop(0, norb)
+        def _(b):
+            send_halos(b, 0)
+
+    @pl.loop(0, ent // TILE)
+    def _(i):
+        part = pl.ds(pl.multiple_of(i * TILE, TILE), TILE)
+        column = cols[part, :]
+        lane = lax.broadcasted_iota(jnp.int32, (TILE, LANES), 1).astype(f32)
+        total = jnp.zeros((TILE, LANES), f32)
+        for j in range(4):
+            total = jnp.where(column[:, 2:3] + (GROUP * j) == lane, column[:, 4 + j : 5 + j], total)
+        high, low = split(total)
+        m_col[part, 0:LANES] = high
+        m_col[part, LANES:] = low
+
+    @pl.loop(0, nx)
+    def _(x):
+        first = pl.multiple_of(x * ny, ny)
+        down = lax.broadcasted_iota(jnp.int32, (ny, ent), 0) + first
+        rows_t[pl.ds(first, ny), :] = jnp.where(down == row_of, 1.0, 0.0).astype(bf16)
+
     coupling_rows()
     loads[4].wait()
 
@@ -406,35 +412,55 @@
 
         along_x(ext1, b, store)
         send_halos(b, 1)
+
+        @pl.when(root & (b == TURN))
+        def _():
+            pl.semaphore_signal(turn_sem, inc=1, device_id=(1, grid), device_id_type=MESH)
+
         coefficients(ext2, b, 1)
 
-    def scatter_copy(b, to):
-        part = pl.ds(pl.multiple_of(to * piece, 8), piece)
-        return pltpu.make_async_remote_copy(
-            src_ref=filt.at[b, part], dst_ref=panel.at[b, part],
-            send_sem=scat_send.at[b, to], recv_sem=scat_recv.at[b],
-            device_id=(2 * to, grid), device_id_type=MESH,
-        )
-
-    def z_copy(b, step):
-        part = pl.ds(pl.multiple_of(chip * piece, 8), piece)
+    def share_of(y):
+        return pl.ds(pl.multiple_of(y * share, 8), share)
+
+    def scatter_copy(b, y):
+        return pltpu.make_async_remote_copy(
+            src_ref=filt.at[b, share_of(y)], dst_ref=panel.at[b, share_of(y)],
+            send_sem=scat_send.at[b, y], recv_sem=scat_recv.at[b],
+            device_id=(2 * n_zh * y, grid), device_id_type=MESH,
+        )
+
+    def z_copy(source, b, way):
+        part = pl.ds(pl.multiple_of(yy * share, 8), share)
+        return pltpu.make_async_remote_copy(
+            src_ref=source.at[b, part], dst_ref=panel.at[b, part],
+            send_sem=z_send.at[b, way], recv_sem=z_recv.at[b, way],
+            device_id=(along_z(n_zh - 1 if way else 1), grid), device_id_type=MESH,
+        )
+
+    def z_relay(b, way):
+        part = pl.ds(pl.multiple_of(yy * share + way * half, 8), half)
         return pltpu.make_async_remote_copy(
             src_ref=panel.at[b, part], dst_ref=panel.at[b, part],
-            send_sem=z_send.at[b, step], recv_sem=z_recv.at[b],
-            device_id=(along_z(step), grid), device_id_type=MESH,
-        )
-
-    def y_copy(b, step):
-        part = pl.ds(pl.multiple_of(yy * share, 8), share)
-        return pltpu.make_async_remote_copy(
-            src_ref=panel.at[b, part], dst_ref=panel.at[b, part],
+            send_sem=z_send.at[b, way], recv_sem=z_recv.at[b, way],
+            device_id=(along_z(n_zh - 1 if way else 1), grid), device_id_type=MESH,
+        )
+
+    def y_copy(source, b, step):
+        return pltpu.make_async_remote_copy(
+            src_ref=source.at[b, share_of(yy)], dst_ref=panel.at[b, share_of(yy)],
             send_sem=y_send.at[b, step], recv_sem=y_recv.at[b],
             device_id=(along_y(step), grid), device_id_type=MESH,
         )
 
-    def sibling_copy(b):
-        return pltpu.make_async_remote_copy(
-            src_ref=panel.at[b], dst_ref=panel.at[b],
+    def y_copies(source, b, act):
+        for step in range(1, n_y):
+            @pl.when(along_y(step) != 0)
+            def _():
+                act(y_copy(source, b, step))
+
+    def sibling_copy(source, b):
+        return pltpu.make_async_remote_copy(
+            src_ref=source.at[b], dst_ref=panel.at[b],
             send_sem=sib_send.at[b], recv_sem=sib_recv.at[b],
             device_id=(sibling, grid), device_id_type=MESH,
         )
@@ -442,64 +468,78 @@
     def self_copy(b):
         return pltpu.make_async_copy(filt.at[b], panel.at[b], copy_sem.at[b])
 
-    def phase_scatter(b):
+    def start(copy):
+        copy.start()
+
+    def root_sends(b):
         @pl.when(root)
         def _():
-            @pl.loop(1, chips)
-            def _(to):
-                scatter_copy(b, to).start()
-
+            for y in range(1, n_y):
+                scatter_copy(b, y).start()
+            if ringed:
+                for way in range(2):
+                    z_copy(filt, b, way).start()
+            y_copies(filt, b, start)
+            sibling_copy(filt, b).start()
             self_copy(b).start()
 
-    def phase_z(b):
-        @pl.when(root)
-        def _():
-            self_copy(b).wait()
-
-        @pl.when(follower)
-        def _():
-            scatter_copy(b, chip).wait_recv()
-
-        @pl.when(main)
-        def _():
-            for step in range(1, n_zh):
-                @pl.when(along_z(step) != 0)
+    def at(z):
+        return follower & (zh == z)
+
+    def phase(k, b):
+        if k == 0:
+            @pl.when(at(0))
+            def _():
+                scatter_copy(b, yy).wait_recv()
+                if ringed:
+                    for way in range(2):
+                        z_copy(panel, b, way).start()
+                y_copies(panel, b, start)
+
+        if k == 1 and ringed:
+            for z, way in ((1, 0), (3, 1)):
+                @pl.when(at(z))
                 def _():
-                    z_copy(b, step).start()
-
-    def phase_y(b):
-        if n_zh > 1:
+                    z_copy(panel, b, way).wait_recv()
+                    z_relay(b, way).start()
+                    y_copies(panel, b, start)
+
+        if k == 2 and ringed:
+            @pl.when(at(2))
+            def _():
+                for way in range(2):
+                    z_relay(b, way).wait_recv()
+                y_copies(panel, b, start)
+
+        if k == 3:
             @pl.when(follower)
             def _():
-                most = panel.at[b, pl.ds(0, share - piece)]
-                pltpu.make_async_copy(most, most, z_recv.at[b]).wait()
-
-        @pl.when(main)
-        def _():
-            for step in range(1, n_y):
-                @pl.when(along_y(step) != 0)
-                def _():
-                    y_copy(b, step).start()
-
-    def phase_sibling(b):
-        if n_y > 1:
-            @pl.when(follower)
+                if n_y > 1:
+                    most = panel.at[b, pl.ds(0, plane_rows - share)]
+                    pltpu.make_async_copy(most, most, y_recv.at[b]).wait()
+                sibling_copy(panel, b).start()
+
+    def slot(t):
+        for k in range(4):
+            b = t - k
+            if isinstance(t, int):
+                if 0 <= b < norb:
+                    phase(k, b)
+                continue
+
+            @pl.when((b >= 0) & (b < norb))
             def _():
-                most = panel.at[b, pl.ds(0, plane_rows - share)]
-                pltpu.make_async_copy(most, most, y_recv.at[b]).wait()
-
-        @pl.when(main)
-        def _():
-            sibling_copy(b).start()
+                phase(k, b)
 
     def phase_last(b):
         @pl.when(core == 1)
         def _():
-            sibling_copy(b).wait_recv()
+            sibling_copy(panel, b).wait_recv()
 
     @pl.loop(0, norb)
     def _(b):
         inner_terms(ext2, b, 1)
+        slot(2 * b - LAG)
         wait_halos(b, 1, False)
 
         def store(x, first, place, total):
@@ -507,26 +547,17 @@
             filt[b, place, :] = 2.0 * total - before
 
         along_x(ext2, b, store)
-        phase_scatter(b)
-
-        @pl.when(b >= 1)
-        def _():
-            phase_z(b - 1)
-
-        @pl.when(b >= 2)
-        def _():
-            phase_y(b - 2)
-
-        @pl.when(b >= 3)
-        def _():
-            phase_sibling(b - 3)
-
-    phase_z(norb - 1)
-    phase_y(norb - 2)
-    phase_sibling(norb - 3)
-    phase_y(norb - 1)
-    phase_sibling(norb - 2)
-    phase_sibling(norb - 1)
+        root_sends(b)
+        slot(2 * b + 1 - LAG)
+
+    for t in range(2 * norb - LAG, norb + 3):
+        slot(t)
+
+    @pl.when(root)
+    def _():
+        for b in range(norb):
+            self_copy(b).wait()
+
     for b in range(norb):
         phase_last(b)
 
@@ -618,25 +649,28 @@
             for d in range(len(COEF_STEPS)):
                 coef_copy(app, b, d).wait_send()
 
+        def ended(copy):
+            copy.wait_send()
+
         @pl.when(root)
         def _():
-            @pl.loop(1, chips)
-            def _(to):
-                scatter_copy(b, to).wait_send()
+            for y in range(1, n_y):
+                scatter_copy(b, y).wait_send()
 
         @pl.when(main)
         def _():
-            for step in range(1, n_zh):
-                @pl.when(along_z(step) != 0)
-                def _():
-                    z_copy(b, step).wait_send()
-
-            for step in range(1, n_y):
-                @pl.when(along_y(step) != 0)
-                def _():
-                    y_copy(b, step).wait_send()
-
-            sibling_copy(b).wait_send()
+            if ringed:
+                for way in range(2):
+                    @pl.when(zh == 0)
+                    def _():
+                        z_copy(panel, b, way).wait_send()
+
+                    @pl.when(zh == (1, 3)[way])
+                    def _():
+                        z_relay(b, way).wait_send()
+
+            y_copies(panel, b, ended)
+            sibling_copy(panel, b).wait_send()
 
     for k in range(2):
         coup_copy(k).wait_send()
@@ -676,7 +710,7 @@
             vmem((ent, 2 * LANES), bf16),
             vmem((ent, 2 * LANES), bf16),
             vmem((norb, rows, 2 * LANES), bf16),
-            vmem((rows, LANES), f32),
+            vmem((norb, rows, LANES), f32),
             vmem((2 * LANES, 2 * LANES), bf16),
             vmem((2 * LANES, 2 * LANES), bf16),
             vmem((ent, 8), f32),
@@ -689,28 +723,29 @@
             vmem((8, LANES), f32),
             vmem((n_grid, 8, LANES), f32),
             dma((5,)),
+            pltpu.SemaphoreType.REGULAR,
             dma((norb,)),
             dma((2, norb, 2)), dma((2, norb, 2)),
             dma((2, norb, 4)), dma((2, norb, 4)),
             dma((2,)), dma((2,)),
-            dma((norb, chips)), dma((norb,)),
             dma((norb, 4)), dma((norb,)),
-            dma((norb, 16)), dma((norb,)),
+            dma((norb, 2)), dma((norb, 2)),
+            dma((norb, 4)), dma((norb,)),
             dma((norb,)), dma((norb,)),
             dma((norb,)),
             dma((n_grid,)), dma((n_grid,)),
         ],
         compiler_params=pltpu.CompilerParams(
-            collective_id=0, has_side_effects=True, vmem_limit_bytes=62 * 1024 * 1024
+            collective_id=0, has_side_effects=True, vmem_limit_bytes=40 * 1024 * 1024
         ),
         name="filter_panel",
     )(
-        orbitals.reshape(norb, rows, nz),
+        *[pltpu.with_memory_space_constraint(v, pltpu.HBM) for v in (orbitals.reshape(norb, rows, nz),
         potential.reshape(rows, nz),
         projectors,
         coupling.transpose(1, 2, 0),
         entry_cell.reshape(1, ent),
-        entry_atom.reshape(1, ent),
+        entry_atom.reshape(1, ent))]
     )
     return out.reshape(orbitals.shape)
 

time: 93.6 us -> 80.6 us (0.86)
  the two profiles are of different devices: /device:TPU:65 before, /device:TPU:129 now
where the time goes in v3:
time: 80.6 us; the launch traced here: 80.5 us
  Pallas kernels  79.4 us (99%)
  local copies, waits for them, and re-layouts  1.06 us (1%)
    pallas_call x1, Pallas kernels, local(): pl.pallas_call(functools.partial(kernel, n_band, n_grid, nx, ny, ent), ou...  79.4 us

profile of v3, /device:TPU:129, one launch (start us, length us, event | category | flops | bytes accessed | tf_op | source)
XLA Modules:
  0.0 80.5 jit_solution(2663289110882205962)
XLA Ops:
  0.0 79.4 %filter_panel.1 = f32[4,640,128]{2,1,0:T(8,128)S(1)} custom-call(f32[4,640,128]{2,1,0:T(8,128)} %bitcast.7, f32[640,128]{1,0:T(8,128)} %bitcast.8, f32[4,2048]{1,0:T(4,128)} %proj_hbm.1, f32[4,4,8]{2,1,0:T(4,128)} %bitcast.9, s32[1,2048]{1,0:T(1,128)} %bitcast.10, s32[1,2048]{1,0:T(1,128)} %bitcast.11), custom_call_target="tpu_custom_call" | custom-call | tf_op jit(solution)/shard_map/filter_panel/pallas_call | solution.py:690
  79.4 1.1 %copy.8 = f32[4,8,80,128]{3,2,1,0:T(8,128)} copy(f32[4,8,80,128]{3,2,1,0:T(8,128)S(1)} %bitcast.6) | data formatting | bytes 2621440

commit v4 on v3

--- a/solution.py
+++ b/solution.py
@@ -16,8 +16,6 @@
 ATOM_DEV = 8
 GROUP = 32
 TILE = 256
-LAG = 1
-TURN = 2
 WIDE = 512
 MESH = pl.DeviceIdType.MESH
 COEF_STEPS = (-2, -1, 1, 2)
@@ -52,10 +50,10 @@
     orb_ref, pot_hbm, proj_hbm, coup_hbm, cell_hbm, atom_hbm,
     out_ref,
     pot_ref, proj_ref, coup_ref, cell_ref, atom_ref,
-    ext1, ext2, filt, panel, rows_m, rows_t, lane_m, m_row, m_col, picked, spread, vcat, acc,
+    ext1, ext2, fields, rows_m, rows_t, lane_m, m_row, m_col, picked, spread, vcat, acc,
     zmat, wcat, cols, coef_out, coef_in, coup_own, coup_in, mix, pairs, gram_out, gram_in,
-    load_sem, turn_sem, own_sem, halo_send, halo_recv, coef_send, coef_recv, coup_send, coup_recv,
-    scat_send, scat_recv, z_send, z_recv, y_send, y_recv, sib_send, sib_recv, copy_sem,
+    load_sem, own_sem, swap_send, back_send, back_recv, halo_send, halo_recv, coef_send, coef_recv, coup_send, coup_recv,
+    scat_send, scat_recv, z_send, z_recv, y_send, y_recv, sib_send, sib_recv,
     gram_send, gram_recv,
 ):
     f32, bf16 = jnp.float32, jnp.bfloat16
@@ -74,6 +72,8 @@
     core = lax.rem(band, 2)
     sibling = band + 1 - 2 * core
     main = core == 0
+    paired = band < 2
+    filt, panel = fields.at[pl.ds(0, norb)], fields.at[pl.ds(norb, norb)]
     has_left, has_right = grid > 0, grid < n_grid - 1
 
     def peer(step):
@@ -107,77 +107,112 @@
     greeted = [along_z(step) for step in (1, n_zh - 1)] if ringed else []
     greeted += [along_y(step) for step in range(1, n_y)]
 
-    @pl.when(main)
+    @pl.when(main | paired)
     def _():
         for to in greeted:
             pl.semaphore_signal(barrier, inc=1, device_id=(to, grid), device_id_type=MESH)
 
-    @pl.when(follower)
+    beside_root = follower & ((zh == 0) | ((yy == 0) & (zh != 2)))
+
+    @pl.when(beside_root)
+    def _():
+        pl.semaphore_signal(barrier, inc=1, device_id=(1, grid), device_id_type=MESH)
+
+    @pl.when(paired)
+    def _():
+        for step in (-1, 1):
+            pl.semaphore_signal(
+                barrier, inc=1, device_id=(sibling, peer(step)), device_id_type=MESH
+            )
+
+    @pl.when(beside_root)
+    def _():
+        pl.semaphore_wait(barrier, n_grid + len(greeted) + 1)
+
+    @pl.when(follower & jnp.logical_not(beside_root))
     def _():
         pl.semaphore_wait(barrier, n_grid + len(greeted))
 
-    @pl.when(core == 1)
+    @pl.when((core == 1) & jnp.logical_not(paired))
     def _():
         pl.semaphore_wait(barrier, n_grid)
 
-    def halo(source, start, ext, b, app, side):
+    def home(o):
+        return jnp.where(paired, o // 2, band), jnp.where(paired, o % 2 + 2 * core, o)
+
+    def halo(b, app, side):
         step = -1 if side == 0 else 1
+        start = 0 if app == 0 else reach_rows
         first = start if side == 0 else start + plane_rows - reach_rows
         land = reach_rows + plane_rows if side == 0 else 0
-        return pltpu.make_async_remote_copy(
-            src_ref=source.at[b, pl.ds(first, reach_rows)],
-            dst_ref=ext.at[b, pl.ds(land, reach_rows)],
+        to_band, place = home(b) if app == 0 else (band, b)
+        return pltpu.make_async_remote_copy(
+            src_ref=(ext2 if app else orb_ref).at[b, pl.ds(first, reach_rows)],
+            dst_ref=(ext2 if app else ext1).at[place, pl.ds(land, reach_rows)],
             send_sem=halo_send.at[app, b, side],
-            recv_sem=halo_recv.at[app, b, 1 - side],
-            device_id=(band, grid + step),
+            recv_sem=halo_recv.at[app, place, 1 - side],
+            device_id=(to_band, grid + step),
             device_id_type=MESH,
         )
 
-    def halo_source(app):
-        return (orb_ref, 0, ext1) if app == 0 else (ext2, reach_rows, ext2)
+    def arrived(b, app, side):
+        ext = ext2 if app else ext1
+        land = 0 if side == 0 else reach_rows + plane_rows
+        there = ext.at[b, pl.ds(land, reach_rows)]
+        return pltpu.make_async_copy(there, there, halo_recv.at[app, b, side])
 
     def send_halos(b, app):
-        source, start, ext = halo_source(app)
-
         @pl.when(has_left)
         def _():
-            halo(source, start, ext, b, app, 0).start()
+            halo(b, app, 0).start()
 
         @pl.when(has_right)
         def _():
-            halo(source, start, ext, b, app, 1).start()
+            halo(b, app, 1).start()
 
     def wait_halos(b, app, sent):
-        source, start, ext = halo_source(app)
-
         @pl.when(has_left)
         def _():
             if sent:
-                halo(source, start, ext, b, app, 0).wait_send()
+                halo(b, app, 0).wait_send()
             else:
-                halo(source, start, ext, b, app, 1).wait_recv()
+                arrived(b, app, 0).wait()
 
         @pl.when(has_right)
         def _():
             if sent:
-                halo(source, start, ext, b, app, 1).wait_send()
+                halo(b, app, 1).wait_send()
             else:
-                halo(source, start, ext, b, app, 0).wait_recv()
+                arrived(b, app, 1).wait()
 
     def own_copy(b):
         return pltpu.make_async_copy(
             orb_ref.at[b], ext1.at[b, pl.ds(reach_rows, plane_rows)], own_sem.at[b]
         )
 
-    waits_turn = band == 1
+    def swap_copy(o):
+        place = home(o)[1]
+        return pltpu.make_async_remote_copy(
+            src_ref=orb_ref.at[o], dst_ref=ext1.at[place, pl.ds(reach_rows, plane_rows)],
+            send_sem=swap_send.at[o], recv_sem=own_sem.at[place],
+            device_id=(sibling, grid), device_id_type=MESH,
+        )
+
+    def stays(o):
+        return home(o)[0] == band
 
     @pl.loop(0, norb)
-    def _(b):
-        own_copy(b).start()
-
-        @pl.when(band > 1)
-        def _():
-            send_halos(b, 0)
+    def _(o):
+        @pl.when(stays(o))
+        def _():
+            place = home(o)[1]
+            pltpu.make_async_copy(
+                orb_ref.at[o], ext1.at[place, pl.ds(reach_rows, plane_rows)], own_sem.at[place]
+            ).start()
+
+        @pl.when(jnp.logical_not(paired))
+        def _():
+            send_halos(o, 0)
 
     for load in loads[:4]:
         load.wait()
@@ -228,13 +263,23 @@
         rows_m[part, :] = jnp.where(column[:, 0:1] == wide, 1.0, 0.0).astype(bf16)
         lane_m[part, :] = jnp.where(column[:, 1:2] == lane, 1.0, 0.0).astype(bf16)
 
+    @pl.when(paired)
+    def _():
+        pl.semaphore_wait(barrier, n_grid + len(greeted) + 2)
+
+        @pl.loop(0, norb)
+        def _(o):
+            @pl.when(root)
+            def _():
+                send_halos(o, 0)
+
+            @pl.when(jnp.logical_not(stays(o)))
+            def _():
+                swap_copy(o).start()
+
     @pl.when(root)
     def _():
-        pl.semaphore_wait(barrier, n_grid + len(greeted))
-
-        @pl.loop(0, norb)
-        def _(b):
-            send_halos(b, 0)
+        filt[0:2] = jnp.zeros((2, plane_rows, LANES), f32)
 
     for k in range(2):
         coup_copy(k).start()
@@ -368,18 +413,13 @@
                     total = total + EK[k - 1] * (cells[x + REACH + k] + cells[x + REACH - k])
                 store(x, first, place, total)
 
-    @pl.loop(0, norb)
-    def _(b):
+    def first_coefficients(b):
         own_copy(b).wait()
         coefficients(ext1, b, 0)
 
-    @pl.when(waits_turn)
-    def _():
-        pl.semaphore_wait(turn_sem, 1)
-
-        @pl.loop(0, norb)
-        def _(b):
-            send_halos(b, 0)
+    @pl.loop(0, jnp.where(paired, 2, norb))
+    def _(b):
+        first_coefficients(b)
 
     @pl.loop(0, ent // TILE)
     def _(i):
@@ -402,8 +442,7 @@
     coupling_rows()
     loads[4].wait()
 
-    @pl.loop(0, norb)
-    def _(b):
+    def first_application(b):
         inner_terms(ext1, b, 0)
         wait_halos(b, 0, False)
 
@@ -411,11 +450,10 @@
             ext2[b, pl.ds(pl.multiple_of(reach_rows + x * ny + first, 8), 8), :] = total
 
         along_x(ext1, b, store)
-        send_halos(b, 1)
-
-        @pl.when(root & (b == TURN))
-        def _():
-            pl.semaphore_signal(turn_sem, inc=1, device_id=(1, grid), device_id_type=MESH)
+
+        @pl.when(jnp.logical_not(follower) | (b == 0))
+        def _():
+            send_halos(b, 1)
 
         coefficients(ext2, b, 1)
 
@@ -424,92 +462,96 @@
 
     def scatter_copy(b, y):
         return pltpu.make_async_remote_copy(
-            src_ref=filt.at[b, share_of(y)], dst_ref=panel.at[b, share_of(y)],
+            src_ref=panel.at[b, share_of(y)], dst_ref=panel.at[b, share_of(y)],
             send_sem=scat_send.at[b, y], recv_sem=scat_recv.at[b],
             device_id=(2 * n_zh * y, grid), device_id_type=MESH,
         )
 
-    def z_copy(source, b, way):
-        part = pl.ds(pl.multiple_of(yy * share, 8), share)
-        return pltpu.make_async_remote_copy(
-            src_ref=source.at[b, part], dst_ref=panel.at[b, part],
+    def z_send_part(b, way, rows):
+        return pltpu.make_async_remote_copy(
+            src_ref=panel.at[b, rows], dst_ref=panel.at[b, rows],
             send_sem=z_send.at[b, way], recv_sem=z_recv.at[b, way],
             device_id=(along_z(n_zh - 1 if way else 1), grid), device_id_type=MESH,
         )
 
+    def z_copy(b, way):
+        return z_send_part(b, way, share_of(yy))
+
     def z_relay(b, way):
-        part = pl.ds(pl.multiple_of(yy * share + way * half, 8), half)
-        return pltpu.make_async_remote_copy(
-            src_ref=panel.at[b, part], dst_ref=panel.at[b, part],
-            send_sem=z_send.at[b, way], recv_sem=z_recv.at[b, way],
-            device_id=(along_z(n_zh - 1 if way else 1), grid), device_id_type=MESH,
-        )
-
-    def y_copy(source, b, step):
-        return pltpu.make_async_remote_copy(
-            src_ref=source.at[b, share_of(yy)], dst_ref=panel.at[b, share_of(yy)],
+        first = pl.multiple_of(yy * share + way * half, 8)
+        return z_send_part(b, way, pl.ds(first, half))
+
+    def y_copy(b, step):
+        return pltpu.make_async_remote_copy(
+            src_ref=panel.at[b, share_of(yy)], dst_ref=panel.at[b, share_of(yy)],
             send_sem=y_send.at[b, step], recv_sem=y_recv.at[b],
             device_id=(along_y(step), grid), device_id_type=MESH,
         )
 
-    def y_copies(source, b, act):
+    def y_copies(b, act):
         for step in range(1, n_y):
             @pl.when(along_y(step) != 0)
             def _():
-                act(y_copy(source, b, step))
-
-    def sibling_copy(source, b):
-        return pltpu.make_async_remote_copy(
-            src_ref=source.at[b], dst_ref=panel.at[b],
+                act(y_copy(b, step))
+
+    def sibling_copy(b):
+        return pltpu.make_async_remote_copy(
+            src_ref=panel.at[b], dst_ref=panel.at[b],
             send_sem=sib_send.at[b], recv_sem=sib_recv.at[b],
             device_id=(sibling, grid), device_id_type=MESH,
         )
 
-    def self_copy(b):
-        return pltpu.make_async_copy(filt.at[b], panel.at[b], copy_sem.at[b])
+    def back_copy(b):
+        return pltpu.make_async_remote_copy(
+            src_ref=filt.at[b + 2], dst_ref=filt.at[b],
+            send_sem=back_send.at[b], recv_sem=back_recv.at[b],
+            device_id=(sibling, grid), device_id_type=MESH,
+        )
 
     def start(copy):
         copy.start()
 
+    def z_copies(b, act):
+        if ringed:
+            for way in range(2):
+                act(z_copy(b, way))
+
     def root_sends(b):
-        @pl.when(root)
-        def _():
+        @pl.when(paired & (b < 2))
+        def _():
+            q = 2 * core + b
             for y in range(1, n_y):
-                scatter_copy(b, y).start()
-            if ringed:
-                for way in range(2):
-                    z_copy(filt, b, way).start()
-            y_copies(filt, b, start)
-            sibling_copy(filt, b).start()
-            self_copy(b).start()
-
-    def at(z):
-        return follower & (zh == z)
+                scatter_copy(q, y).start()
+            z_copies(q, start)
+            y_copies(q, start)
+            sibling_copy(q).start()
+
+        @pl.when(root & (b >= 2))
+        def _():
+            back_copy(b - 2).start()
 
     def phase(k, b):
         if k == 0:
-            @pl.when(at(0))
+            @pl.when(follower & (zh == 0))
             def _():
                 scatter_copy(b, yy).wait_recv()
-                if ringed:
-                    for way in range(2):
-                        z_copy(panel, b, way).start()
-                y_copies(panel, b, start)
+                z_copies(b, start)
+                y_copies(b, start)
 
         if k == 1 and ringed:
             for z, way in ((1, 0), (3, 1)):
-                @pl.when(at(z))
+                @pl.when(follower & (zh == z))
                 def _():
-                    z_copy(panel, b, way).wait_recv()
+                    z_copy(b, way).wait_recv()
                     z_relay(b, way).start()
-                    y_copies(panel, b, start)
+                    y_copies(b, start)
 
         if k == 2 and ringed:
-            @pl.when(at(2))
+            @pl.when(follower & (zh == 2))
             def _():
                 for way in range(2):
                     z_relay(b, way).wait_recv()
-                y_copies(panel, b, start)
+                y_copies(b, start)
 
         if k == 3:
             @pl.when(follower)
@@ -517,49 +559,66 @@
                 if n_y > 1:
                     most = panel.at[b, pl.ds(0, plane_rows - share)]
                     pltpu.make_async_copy(most, most, y_recv.at[b]).wait()
-                sibling_copy(panel, b).start()
-
-    def slot(t):
+                sibling_copy(b).start()
+
+    def hand_on(b):
         for k in range(4):
-            b = t - k
-            if isinstance(t, int):
-                if 0 <= b < norb:
-                    phase(k, b)
-                continue
-
-            @pl.when((b >= 0) & (b < norb))
+            @pl.when(follower & (b == k))
             def _():
-                phase(k, b)
-
-    def phase_last(b):
-        @pl.when(core == 1)
-        def _():
-            sibling_copy(panel, b).wait_recv()
-
-    @pl.loop(0, norb)
-    def _(b):
+                for q in (0, 2, 1, 3):
+                    phase(k, q)
+                if k < 3:
+                    send_halos(k + 1, 1)
+
+    def second_application(b):
         inner_terms(ext2, b, 1)
-        slot(2 * b - LAG)
+        hand_on(b)
         wait_halos(b, 1, False)
+        target = jnp.where(paired & (b < 2), norb + 2 * core + b, b)
 
         def store(x, first, place, total):
             before = ext1[b, pl.ds(pl.multiple_of(reach_rows + x * ny + first, 8), 8), :]
-            filt[b, place, :] = 2.0 * total - before
+            fields[target, place, :] = 2.0 * total - before
 
         along_x(ext2, b, store)
         root_sends(b)
-        slot(2 * b + 1 - LAG)
-
-    for t in range(2 * norb - LAG, norb + 3):
-        slot(t)
-
-    @pl.when(root)
+
+        @pl.when(paired & (b == 1))
+        def _():
+            @pl.when(core == 1)
+            def _():
+                @pl.loop(0, norb)
+                def _(o):
+                    send_halos(o, 0)
+
+            @pl.loop(2, norb)
+            def _(late):
+                first_coefficients(late)
+
+    @pl.loop(0, 2 * norb)
+    def _(i):
+        first = jnp.where(paired, i % 4 < 2, i < norb)
+        b = jnp.where(paired, i // 4 * 2 + i % 2, i % norb)
+
+        @pl.when(first)
+        def _():
+            first_application(b)
+
+        @pl.when(jnp.logical_not(first))
+        def _():
+            second_application(b)
+
+    for b in range(norb):
+        given = (core == 1) & jnp.logical_not(paired) | paired & (core != b // 2)
+
+        @pl.when(given)
+        def _():
+            sibling_copy(b).wait_recv()
+
+    @pl.when(band == 1)
     def _():
-        for b in range(norb):
-            self_copy(b).wait()
-
-    for b in range(norb):
-        phase_last(b)
+        for b in range(2):
+            back_copy(b).wait_recv()
 
     couples = [(k, m) for k in range(norb) for m in range(k + 1)]
     n_pairs = len(couples) + norb * norb
@@ -652,25 +711,36 @@
         def ended(copy):
             copy.wait_send()
 
-        @pl.when(root)
+        @pl.when(paired & (core == b // 2))
         def _():
             for y in range(1, n_y):
                 scatter_copy(b, y).wait_send()
-
-        @pl.when(main)
-        def _():
+            z_copies(b, ended)
+            y_copies(b, ended)
+            sibling_copy(b).wait_send()
+
+        @pl.when(follower)
+        def _():
+            @pl.when(zh == 0)
+            def _():
+                z_copies(b, ended)
+
             if ringed:
-                for way in range(2):
-                    @pl.when(zh == 0)
-                    def _():
-                        z_copy(panel, b, way).wait_send()
-
-                    @pl.when(zh == (1, 3)[way])
+                for z, way in ((1, 0), (3, 1)):
+                    @pl.when(zh == z)
                     def _():
                         z_relay(b, way).wait_send()
 
-            y_copies(panel, b, ended)
-            sibling_copy(panel, b).wait_send()
+            y_copies(b, ended)
+            sibling_copy(b).wait_send()
+
+        @pl.when(jnp.logical_not(stays(b)))
+        def _():
+            swap_copy(b).wait_send()
+
+        @pl.when(root & (b < 2))
+        def _():
+            back_copy(b).wait_send()
 
     for k in range(2):
         coup_copy(k).wait_send()
@@ -700,8 +770,7 @@
             vmem((1, ent), jnp.int32),
             vmem((norb, ext_rows, nz), f32),
             vmem((norb, ext_rows, nz), f32),
-            vmem((norb, rows, nz), f32),
-            vmem((norb, rows, nz), f32),
+            vmem((2 * norb, rows, nz), f32),
             vmem((ent, rows), bf16),
             vmem((rows, ent), bf16),
             vmem((ent, LANES), bf16),
@@ -723,8 +792,8 @@
             vmem((8, LANES), f32),
             vmem((n_grid, 8, LANES), f32),
             dma((5,)),
-            pltpu.SemaphoreType.REGULAR,
             dma((norb,)),
+            dma((norb,)), dma((2,)), dma((2,)),
             dma((2, norb, 2)), dma((2, norb, 2)),
             dma((2, norb, 4)), dma((2, norb, 4)),
             dma((2,)), dma((2,)),
@@ -732,7 +801,6 @@
             dma((norb, 2)), dma((norb, 2)),
             dma((norb, 4)), dma((norb,)),
             dma((norb,)), dma((norb,)),
-            dma((norb,)),
             dma((n_grid,)), dma((n_grid,)),
         ],
         compiler_params=pltpu.CompilerParams(

time: 80.6 us -> 77.4 us (0.960)
  Pallas kernels: 79.4 us -> 75.8 us
    pallas_call x1, Pallas kernels: 79.4 us -> 75.8 us  [local(): pl.pallas_call(functools.partial(kernel, n_band, n_grid, nx, ny, ent), ou...]
where the time goes in v4:
time: 77.4 us; the launch traced here: 76.8 us
  Pallas kernels  75.8 us (98%)
  local copies, waits for them, and re-layouts  1.06 us (1%)
    pallas_call x1, Pallas kernels, local(): pl.pallas_call(functools.partial(kernel, n_band, n_grid, nx, ny, ent), ou...  75.8 us

profile of v4, /device:TPU:129, one launch (start us, length us, event | category | flops | bytes accessed | tf_op | source)
XLA Modules:
  0.0 76.8 jit_solution(2229780082590368819)
XLA Ops:
  0.0 75.8 %filter_panel.1 = f32[4,640,128]{2,1,0:T(8,128)S(1)} custom-call(f32[4,640,128]{2,1,0:T(8,128)} %bitcast.7, f32[640,128]{1,0:T(8,128)} %bitcast.8, f32[4,2048]{1,0:T(4,128)} %proj_hbm.1, f32[4,4,8]{2,1,0:T(4,128)} %bitcast.9, s32[1,2048]{1,0:T(1,128)} %bitcast.10, s32[1,2048]{1,0:T(1,128)} %bitcast.11), custom_call_target="tpu_custom_call" | custom-call | tf_op jit(solution)/shard_map/filter_panel/pallas_call | solution.py:760
  75.8 1.1 %copy.8 = f32[4,8,80,128]{3,2,1,0:T(8,128)} copy(f32[4,8,80,128]{3,2,1,0:T(8,128)S(1)} %bitcast.6) | data formatting | bytes 2621440

commit v5 on v4

--- a/solution.py
+++ b/solution.py
@@ -53,7 +53,7 @@
     ext1, ext2, fields, rows_m, rows_t, lane_m, m_row, m_col, picked, spread, vcat, acc,
     zmat, wcat, cols, coef_out, coef_in, coup_own, coup_in, mix, pairs, gram_out, gram_in,
     load_sem, own_sem, swap_send, back_send, back_recv, halo_send, halo_recv, coef_send, coef_recv, coup_send, coup_recv,
-    scat_send, scat_recv, z_send, z_recv, y_send, y_recv, sib_send, sib_recv,
+    scat_send, scat_recv, z_send, z_recv, z2_send, z2_recv, y_send, y_recv, sib_send, sib_recv,
     gram_send, gram_recv,
 ):
     f32, bf16 = jnp.float32, jnp.bfloat16
@@ -451,7 +451,7 @@
 
         along_x(ext1, b, store)
 
-        @pl.when(jnp.logical_not(follower) | (b == 0))
+        @pl.when(jnp.logical_not(follower) | (zh == 2) | (b == 0) | ((zh != 0) & (b == 1)))
         def _():
             send_halos(b, 1)
 
@@ -467,19 +467,20 @@
             device_id=(2 * n_zh * y, grid), device_id_type=MESH,
         )
 
-    def z_send_part(b, way, rows):
+    def z_part(b, way, part, sent, got):
+        first = pl.multiple_of(yy * share + part * half, 8)
+        rows = pl.ds(first, half)
         return pltpu.make_async_remote_copy(
             src_ref=panel.at[b, rows], dst_ref=panel.at[b, rows],
-            send_sem=z_send.at[b, way], recv_sem=z_recv.at[b, way],
+            send_sem=sent.at[b, way], recv_sem=got.at[b, way],
             device_id=(along_z(n_zh - 1 if way else 1), grid), device_id_type=MESH,
         )
 
     def z_copy(b, way):
-        return z_send_part(b, way, share_of(yy))
-
-    def z_relay(b, way):
-        first = pl.multiple_of(yy * share + way * half, 8)
-        return z_send_part(b, way, pl.ds(first, half))
+        return z_part(b, way, way, z_send, z_recv)
+
+    def z_second(b, way):
+        return z_part(b, way, 1 - way, z2_send, z2_recv)
 
     def y_copy(b, step):
         return pltpu.make_async_remote_copy(
@@ -515,6 +516,8 @@
         if ringed:
             for way in range(2):
                 act(z_copy(b, way))
+            for way in range(2):
+                act(z_second(b, way))
 
     def root_sends(b):
         @pl.when(paired & (b < 2))
@@ -530,49 +533,59 @@
         def _():
             back_copy(b - 2).start()
 
-    def phase(k, b):
-        if k == 0:
-            @pl.when(follower & (zh == 0))
+    turns = (0, 2, 1, 3)
+
+    def hand_on_first(b):
+        @pl.when(follower & (zh == 0) & (b == 0))
+        def _():
+            for q in turns:
+                scatter_copy(q, yy).wait_recv()
+                if ringed:
+                    for way in range(2):
+                        z_copy(q, way).start()
+            if ringed:
+                for q in turns:
+                    for way in range(2):
+                        z_second(q, way).start()
+            for late in range(1, norb):
+                send_halos(late, 1)
+            for q in turns:
+                y_copies(q, start)
+
+    def hand_on_next(b):
+        if ringed:
+            for z, way in ((1, 0), (3, 1)):
+                @pl.when(follower & (zh == z) & (b == 0))
+                def _():
+                    for q in turns:
+                        z_copy(q, way).wait_recv()
+                        z_copy(q, way).start()
+                    for late in range(2, norb):
+                        send_halos(late, 1)
+                    for q in turns:
+                        z_second(q, way).wait_recv()
+                        y_copies(q, start)
+
+            @pl.when(follower & (zh == 2) & (b == 1))
             def _():
-                scatter_copy(b, yy).wait_recv()
-                z_copies(b, start)
-                y_copies(b, start)
-
-        if k == 1 and ringed:
-            for z, way in ((1, 0), (3, 1)):
-                @pl.when(follower & (zh == z))
-                def _():
-                    z_copy(b, way).wait_recv()
-                    z_relay(b, way).start()
-                    y_copies(b, start)
-
-        if k == 2 and ringed:
-            @pl.when(follower & (zh == 2))
-            def _():
-                for way in range(2):
-                    z_relay(b, way).wait_recv()
-                y_copies(b, start)
-
-        if k == 3:
-            @pl.when(follower)
-            def _():
+                for q in turns:
+                    for way in range(2):
+                        z_copy(q, way).wait_recv()
+                    y_copies(q, start)
+
+    def hand_on_last(b):
+        @pl.when(follower & (b == 3))
+        def _():
+            for q in turns:
                 if n_y > 1:
-                    most = panel.at[b, pl.ds(0, plane_rows - share)]
-                    pltpu.make_async_copy(most, most, y_recv.at[b]).wait()
-                sibling_copy(b).start()
-
-    def hand_on(b):
-        for k in range(4):
-            @pl.when(follower & (b == k))
-            def _():
-                for q in (0, 2, 1, 3):
-                    phase(k, q)
-                if k < 3:
-                    send_halos(k + 1, 1)
+                    most = panel.at[q, pl.ds(0, plane_rows - share)]
+                    pltpu.make_async_copy(most, most, y_recv.at[q]).wait()
+                sibling_copy(q).start()
 
     def second_application(b):
+        hand_on_first(b)
         inner_terms(ext2, b, 1)
-        hand_on(b)
+        hand_on_last(b)
         wait_halos(b, 1, False)
         target = jnp.where(paired & (b < 2), norb + 2 * core + b, b)
 
@@ -582,6 +595,7 @@
 
         along_x(ext2, b, store)
         root_sends(b)
+        hand_on_next(b)
 
         @pl.when(paired & (b == 1))
         def _():
@@ -729,7 +743,7 @@
                 for z, way in ((1, 0), (3, 1)):
                     @pl.when(zh == z)
                     def _():
-                        z_relay(b, way).wait_send()
+                        z_copy(b, way).wait_send()
 
             y_copies(b, ended)
             sibling_copy(b).wait_send()
@@ -799,6 +813,7 @@
             dma((2,)), dma((2,)),
             dma((norb, 4)), dma((norb,)),
             dma((norb, 2)), dma((norb, 2)),
+            dma((norb, 2)), dma((norb, 2)),
             dma((norb, 4)), dma((norb,)),
             dma((norb,)), dma((norb,)),
             dma((n_grid,)), dma((n_grid,)),

time: 77.4 us -> 75.5 us (0.975)
  Pallas kernels: 75.8 us -> 74.3 us
    pallas_call x1, Pallas kernels: 75.8 us -> 74.3 us  [local(): pl.pallas_call(functools.partial(kernel, n_band, n_grid, nx, ny, ent), ou...]
where the time goes in v5:
time: 75.5 us; the launch traced here: 75.3 us
  Pallas kernels  74.3 us (98%)
  local copies, waits for them, and re-layouts  1.06 us (1%)
    pallas_call x1, Pallas kernels, local(): pl.pallas_call(functools.partial(kernel, n_band, n_grid, nx, ny, ent), ou...  74.3 us

profile of v5, /device:TPU:129, one launch (start us, length us, event | category | flops | bytes accessed | tf_op | source)
XLA Modules:
  0.0 75.3 jit_solution(14425904934787230258)
XLA Ops:
  0.0 74.3 %filter_panel.1 = f32[4,640,128]{2,1,0:T(8,128)S(1)} custom-call(f32[4,640,128]{2,1,0:T(8,128)} %bitcast.7, f32[640,128]{1,0:T(8,128)} %bitcast.8, f32[4,2048]{1,0:T(4,128)} %proj_hbm.1, f32[4,4,8]{2,1,0:T(4,128)} %bitcast.9, s32[1,2048]{1,0:T(1,128)} %bitcast.10, s32[1,2048]{1,0:T(1,128)} %bitcast.11), custom_call_target="tpu_custom_call" | custom-call | tf_op jit(solution)/shard_map/filter_panel/pallas_call | solution.py:774
  74.3 1.1 %copy.8 = f32[4,8,80,128]{3,2,1,0:T(8,128)} copy(f32[4,8,80,128]{3,2,1,0:T(8,128)S(1)} %bitcast.6) | data formatting | bytes 2621440

commit v6 on v5

--- a/solution.py
+++ b/solution.py
@@ -451,7 +451,7 @@
 
         along_x(ext1, b, store)
 
-        @pl.when(jnp.logical_not(follower) | (zh == 2) | (b == 0) | ((zh != 0) & (b == 1)))
+        @pl.when(jnp.logical_not(follower) | ((zh == 2) & (b < 3)) | (b == 0) | ((zh != 0) & (b == 1)))
         def _():
             send_halos(b, 1)
 
@@ -490,7 +490,7 @@
         )
 
     def y_copies(b, act):
-        for step in range(1, n_y):
+        for step in sorted(range(1, n_y), key=lambda step: abs(2 * step - n_y)):
             @pl.when(along_y(step) != 0)
             def _():
                 act(y_copy(b, step))
@@ -572,6 +572,7 @@
                     for way in range(2):
                         z_copy(q, way).wait_recv()
                     y_copies(q, start)
+                send_halos(3, 1)
 
     def hand_on_last(b):
         @pl.when(follower & (b == 3))

time: 75.5 us -> 75.3 us (level)
  no operation moved by 1% of the time
where the time goes in v6:
time: 75.3 us; the launch traced here: 75.2 us
  Pallas kernels  74.1 us (98%)
  local copies, waits for them, and re-layouts  1.06 us (1%)
    pallas_call x1, Pallas kernels, local(): pl.pallas_call(functools.partial(kernel, n_band, n_grid, nx, ny, ent), ou...  74.1 us

profile of v6, /device:TPU:129, one launch (start us, length us, event | category | flops | bytes accessed | tf_op | source)
XLA Modules:
  0.0 75.2 jit_solution(7818910445918010221)
XLA Ops:
  0.0 74.1 %filter_panel.1 = f32[4,640,128]{2,1,0:T(8,128)S(1)} custom-call(f32[4,640,128]{2,1,0:T(8,128)} %bitcast.7, f32[640,128]{1,0:T(8,128)} %bitcast.8, f32[4,2048]{1,0:T(4,128)} %proj_hbm.1, f32[4,4,8]{2,1,0:T(4,128)} %bitcast.9, s32[1,2048]{1,0:T(1,128)} %bitcast.10, s32[1,2048]{1,0:T(1,128)} %bitcast.11), custom_call_target="tpu_custom_call" | custom-call | tf_op jit(solution)/shard_map/filter_panel/pallas_call | solution.py:775
  74.1 1.1 %copy.8 = f32[4,8,80,128]{3,2,1,0:T(8,128)} copy(f32[4,8,80,128]{3,2,1,0:T(8,128)S(1)} %bitcast.6) | data formatting | bytes 2621440
